TPU v7x, 32 devices: a whole 2x2x4 slice. The times are simulated.
32 devices in a mesh: ctx: 8 (over y, x, core), ts: 4 (over z).
Axes of the slice: x: 2, y: 2, z: 4, core: 2. Of those that a mesh axis runs over, the one named last changes fastest.
Arguments:
- projected: bfloat16 [4096, 12288], P(('ctx', 'ts')), may hold values from -6 to 6
- doc_lengths: int32 [16], replicated, may hold values from 1 to 1024, 4096 in all
- short_taps: float32 [3, 7, 256], replicated, may hold values from -2.4 to 2.4
- medium_taps: float32 [128, 256], replicated, may hold values from -0.5 to 0.5
- decay_rates: float32 [16, 256], replicated, may hold values from 6.1035156e-05 to 0.03
- residues: float32 [16, 256], replicated, may hold values from -1.5 to 1.5
- skip_gain: float32 [4096], replicated, may hold values from -3 to 3
Outputs:
- hyena_out: bfloat16 [4096, 4096], P(('ctx', 'ts'))
Inputs may be any that keep to these rules, and one draw needn't show every extreme that they name: `doc_lengths`: the lengths sum to 4096; the largest is exactly 1024.
All inputs are finite; a program needn't handle non-finite values.
Results may differ from a plain program's by a relative error of at most 0.01.
Values may be sent and summed in bfloat16 or wider, within the bound.
A program may use at most 128 MiB of HBM per device.

v0:
```python
import jax
import jax.numpy as jnp
from jax import lax
from jax.sharding import PartitionSpec as P

GROUP = 16
SHORT = 7
MEDIUM = 128
MODES = 16


HIGHEST = lax.Precision.HIGHEST


def from_behind(value, axis, by):
    length = lax.axis_size(axis)
    pairs = [(i, i + by) for i in range(length) if 0 <= i + by < length]
    return lax.ppermute(value, axis, pairs)


def carried_in(part, axis, combine, identity):
    place = lax.axis_index(axis)
    gathered = jax.tree.map(lambda a: lax.all_gather(a, axis), part)
    state = jax.tree.map(lambda a, e: jnp.zeros_like(a) + jnp.asarray(e, a.dtype), part, identity)

    def one(turn, state):
        return combine(
            state, jax.tree.map(lambda a: lax.dynamic_index_in_dim(a, turn, 0, False), gathered)
        )

    return lax.fori_loop(0, place, one, state)


def starts_for(positions, doc_lengths):
    doc_ends = jnp.cumsum(doc_lengths)
    doc_begins = doc_ends - doc_lengths
    inside = doc_begins[None, :] <= positions[:, None]
    return jnp.max(jnp.where(inside, doc_begins[None, :], 0), axis=1)


def featurize(window, positions, row_start, tap_table):
    row_count = positions.shape[0]
    summed = jnp.zeros((row_count,) + window.shape[1:], jnp.float32)
    for offset in range(SHORT):
        in_doc = positions - offset >= row_start
        shifted = window[SHORT - 1 - offset : SHORT - 1 - offset + row_count]
        summed = summed + jnp.where(
            in_doc[:, None, None], shifted * tap_table[:, offset][None], 0.0
        )
    return summed


def filter_tables(decay_rates, residues):
    scaled = residues * jnp.sqrt(-jnp.expm1(-2.0 * decay_rates))
    steps_f = jnp.arange(MEDIUM).astype(jnp.float32)
    long_table = jnp.sum(
        scaled[None] * jnp.exp(-decay_rates[None] * steps_f[:, None, None]), axis=1
    )
    return (scaled, long_table)


def band_matrix(medium_taps, long_table, row_pos, col_pos, block_begin):
    distance = row_pos[:, None] - col_pos[None, :]
    in_band = (distance >= 0) & (distance < MEDIUM)
    lag_index = jnp.clip(distance, 0, MEDIUM - 1)
    same_block = (col_pos >= block_begin)[None, :, None]
    tap_values = medium_taps[lag_index] + jnp.where(same_block, long_table[lag_index], 0.0)
    return jnp.where(in_band[:, :, None], tap_values, 0.0)


def split_pieces(matrix):
    upper = matrix.astype(jnp.bfloat16)
    rest = matrix - upper.astype(jnp.float32)
    middle = rest.astype(jnp.bfloat16)
    lower = (rest - middle.astype(jnp.float32)).astype(jnp.bfloat16)
    return jnp.stack([upper, middle, lower], axis=0)


def combine(earlier, later):
    return (earlier[0] * later[0], later[0] * earlier[1] + later[1])


def per_device(projected, doc_lengths, short_taps, medium_taps, decay_rates, residues, skip_gain):
    ts_count = lax.axis_size("ts")
    ts_index = lax.axis_index("ts")
    ctx_index = lax.axis_index("ctx")
    tok_rows = projected.shape[0]
    width = projected.shape[1] // 3
    span_rows = tok_rows * ts_count
    local_width = width // ts_count
    local_groups = local_width // GROUP
    blocks_dev = span_rows // MEDIUM
    group_begin = ts_index * local_groups
    my_medium = lax.dynamic_slice_in_dim(medium_taps, group_begin, local_groups, 1)
    my_rates = lax.dynamic_slice_in_dim(decay_rates, group_begin, local_groups, 1)
    my_residues = lax.dynamic_slice_in_dim(residues, group_begin, local_groups, 1)
    my_skip = lax.dynamic_slice_in_dim(skip_gain, ts_index * local_width, local_width, 0)
    scaled, long_table = filter_tables(my_rates, my_residues)
    span_begin = ctx_index * span_rows
    chan_pos = span_begin + jnp.arange(span_rows, dtype=jnp.int32)
    chan_start = starts_for(chan_pos, doc_lengths)
    stacked = projected.reshape(tok_rows, 3, width)
    switched = lax.all_to_all(stacked, "ts", split_axis=2, concat_axis=0, tiled=True)
    edge_raw = from_behind(switched[span_rows - (SHORT - 1) :], "ctx", 1)
    my_short = jnp.repeat(
        lax.dynamic_slice_in_dim(short_taps, group_begin, local_groups, 2), GROUP, axis=2
    )
    window = jnp.concatenate([edge_raw, switched], axis=0).astype(jnp.float32)
    feature = featurize(window, chan_pos, chan_start, my_short)
    query = feature[:, 0]
    product = (feature[:, 1] * feature[:, 2]).astype(jnp.bfloat16)
    edge_rows = from_behind(product[span_rows - MEDIUM :], "ctx", 1)
    extended = jnp.concatenate([edge_rows, product], axis=0)
    rel_rows = MEDIUM + jnp.arange(MEDIUM, dtype=jnp.int32)
    rel_cols = jnp.arange(2 * MEDIUM, dtype=jnp.int32)
    pieces = split_pieces(band_matrix(my_medium, long_table, rel_rows, rel_cols, MEDIUM))
    local_f = jnp.arange(MEDIUM).astype(jnp.float32)
    decay_rows = scaled[None] * jnp.exp(-my_rates[None] * (local_f + 1.0)[:, None, None])
    tail_power = jnp.exp(-my_rates[None] * (MEDIUM - 1.0 - local_f)[:, None, None])
    block_decay = jnp.exp(-my_rates * MEDIUM)
    product_f = product.astype(jnp.float32).reshape(blocks_dev, MEDIUM, local_width)
    start_rows = chan_start.reshape(blocks_dev, MEDIUM)
    pos_rows = chan_pos.reshape(blocks_dev, MEDIUM)
    begins_dev = pos_rows[:, 0]
    last_start = start_rows[:, MEDIUM - 1]
    kept_rows = jnp.where((pos_rows >= last_start[:, None])[:, :, None], product_f, 0.0)
    kept_rows = kept_rows.reshape(blocks_dev, MEDIUM, local_groups, GROUP)
    contribution = jnp.einsum("umg,bugc->bmgc", tail_power, kept_rows, precision=HIGHEST).reshape(
        blocks_dev, MODES, local_width
    )
    factors = jnp.where((last_start < begins_dev)[:, None, None], block_decay[None], 0.0)
    factors = jnp.repeat(factors, GROUP, axis=2)

    def local_step(carry_pair, inputs):
        decay_acc, state_acc = carry_pair
        factor, term = inputs
        decay_acc = factor * decay_acc
        state_acc = factor * state_acc + term
        return ((decay_acc, state_acc), (decay_acc, state_acc))

    ones_state = jnp.ones((MODES, local_width), jnp.float32)
    zero_state = jnp.zeros((MODES, local_width), jnp.float32)
    finals, stacks = lax.scan(local_step, (ones_state, zero_state), (factors, contribution))
    decay_cum, state_loc = stacks
    total_decay = decay_cum[blocks_dev - 1]
    total_state = state_loc[blocks_dev - 1]

    def block_filter(block_idx):
        block_begin = span_begin + block_idx * MEDIUM
        row_pos = block_begin + jnp.arange(MEDIUM, dtype=jnp.int32)
        row_start = starts_for(row_pos, doc_lengths)
        col_pos = block_begin - MEDIUM + rel_cols
        allowed = col_pos[None, :] >= row_start[:, None]
        masked = jnp.where(allowed[None, :, :, None], pieces, jnp.zeros((), jnp.bfloat16))
        window_x = lax.dynamic_slice_in_dim(extended, block_idx * MEDIUM, 2 * MEDIUM, 0)
        window_x = window_x.reshape(2 * MEDIUM, local_groups, GROUP)
        return jnp.einsum(
            "ptug,ugc->tgc", masked, window_x, preferred_element_type=jnp.float32
        ).reshape(MEDIUM, local_width)

    banded = lax.map(block_filter, jnp.arange(blocks_dev, dtype=jnp.int32))
    prefix = carried_in((total_decay, total_state), "ctx", combine, (ones_state, zero_state))
    state_in = prefix[1]
    previous_states = jnp.concatenate([zero_state[None], state_loc[: blocks_dev - 1]], axis=0)
    previous_states = (
        previous_states
        + jnp.concatenate([ones_state[None], decay_cum[: blocks_dev - 1]], axis=0) * state_in[None]
    )
    carried_part = jnp.einsum(
        "tmg,bmgc->btgc",
        decay_rows,
        previous_states.reshape(blocks_dev, MODES, local_groups, GROUP),
        precision=HIGHEST,
    )
    carried_part = carried_part.reshape(blocks_dev, MEDIUM, local_width)
    carried_part = jnp.where((start_rows < begins_dev[:, None])[:, :, None], carried_part, 0.0)
    filtered = (
        (banded + carried_part + my_skip[None, None, :] * product_f)
        .reshape(span_rows, local_width)
        .astype(jnp.bfloat16)
    )
    outgoing = (query * filtered.astype(jnp.float32)).astype(jnp.bfloat16)
    returned = lax.all_to_all(outgoing, "ts", split_axis=0, concat_axis=1, tiled=True)
    return returned


def solution(mesh):
    return jax.shard_map(
        per_device,
        mesh=mesh,
        in_specs=(P(("ctx", "ts"), None), P(), P(), P(), P(), P(), P()),
        out_specs=P(("ctx", "ts"), None),
        check_vma=False,
    )
```

profile of v0, /device:TPU:1, one launch (start us, length us, event | category | flops | bytes accessed | tf_op | source)
XLA Modules:
  0.0 573.7 jit_solution(14053433864649303085)
XLA Ops:
  0.0 3.5 copy.112
  3.5 20.5 %copy.113 = bf16[128,3,4096]{0,1,2:T(4,128)(2,1)} copy(bf16[128,3,4096]{0,2,1:T(8,128)(2,1)S(1)} %bitcast.122) | data formatting | bytes 6291456 | tf_op jit(solution)/shard_map/reshape | solution.py:102
  24.0 6.1 %all-to-all-start = ((bf16[128,3,4096]{0,1,2:T(4,128)(2,1)}), bf16[128,3,4096]{0,1,2:T(4,128)(2,1)}, u32[]{:S(2)}, u32[]{:S(2)}) async-start(bf16[128,3,4096]{0,1,2:T(4,128)(2,1)} %copy.113), calls=%async_computation | async-start | bytes 8388608 | tf_op jit(solution)/shard_map/all_to_all | solution.py:103
  32.3 108.4 %gather_fusion = f32[32768,64]{1,0:T(8,128)} fusion(f32[128,64]{1,0:T(8,128)S(1)} %constant_dynamic-slice_fusion.1, s32[32768]{0:T(1024)S(1)} %broadcast_clamp_fusion), kind=kCustom, calls=%fused_computation | custom fusion | bytes 16908288 | tf_op jit(solution)/shard_map/gather | solution.py:67
  140.7 12.8 %copy.122 = f32[1,128,256,64]{2,3,1,0:T(8,128)} copy(f32[1,128,256,64]{3,2,1,0:T(8,128)} %bitcast.116) | data formatting | bytes 16777216 | tf_op jit(solution)/shard_map/gather | solution.py:67
  153.6 108.4 %gather_fusion.1 = f32[32768,64]{1,0:T(8,128)} fusion(f32[128,64]{1,0:T(8,128)S(1)} %copy.119, s32[32768]{0:T(1024)S(1)} %broadcast_clamp_fusion), kind=kCustom, calls=%fused_computation.1 | custom fusion | bytes 16908288 | tf_op jit(solution)/shard_map/gather | solution.py:67
  261.9 12.7 %copy.121 = f32[1,128,256,64]{2,3,1,0:T(8,128)} copy(f32[1,128,256,64]{3,2,1,0:T(8,128)} %bitcast.115) | data formatting | bytes 16777216 | tf_op jit(solution)/shard_map/gather | solution.py:67
  275.2 0.6 broadcast_compare_fusion.1
  279.2 13.6 %fusion.44 = (bf16[1,128,256,64]{2,3,1,0:T(8,128)(2,1)}, f32[1,128,256,64]{2,3,1,0:T(8,128)}) fusion(f32[1,128,256,64]{2,3,1,0:T(8,128)} %copy.122, f32[1,128,256,64]{2,3,1,0:T(8,128)} %copy.121, pred[256]{0:T(512)(128)(4,1)S(1)} %iota_compare_fusion, pred[128,256]{1,0:T(8,128)(4,1)S(1)} %fusion.42), kind=kLoop, calls=%fused_computation.109 | loop fusion | flops 8388608 | bytes 29393152 | tf_op jit(solution)/shard_map/convert_element_type | solution.py:72
  292.9 8.3 %fusion.15 = (bf16[1,128,256,64]{2,3,1,0:T(8,128)(2,1)S(1)}, bf16[1,128,256,64]{2,3,1,0:T(8,128)(2,1)S(1)}) fusion(f32[1,128,256,64]{2,3,1,0:T(8,128)} %get-tuple-element.322), kind=kLoop, calls=%fused_computation.41 | loop fusion | flops 14680064 | bytes 16777216 | tf_op jit(solution)/shard_map/convert_element_type | solution.py:74
  301.2 5.6 pad_maximum_fusion
  306.8 4.3 copy.114
  311.1 3.2 copy.115
  314.3 0.6 slice.111
  314.9 3.9 collective-permute-start
  320.0 23.1 %copy.125 = bf16[3,128,256,64]{3,2,1,0:T(8,128)(2,1)} copy(bf16[3,128,256,64]{2,3,1,0:T(8,128)(2,1)} %pad_maximum_fusion) | data formatting | bytes 25165824
  343.1 2.0 broadcast_in_dim.235
  345.1 3.1 reshape.393
  348.4 1.7 maximum_convert_fusion
  350.2 8.8 %fusion.3 = f32[512,3,1024]{2,0,1:T(8,128)S(1)} fusion(f32[518,3,1024]{2,0,1:T(8,128)S(1)} %maximum_convert_fusion, f32[3,1024]{1,0:T(4,128)S(1)} %get-tuple-element.345, f32[3,1024]{1,0:T(4,128)S(1)} %copy-done.8, f32[3,1024]{1,0:T(4,128)S(1)} %copy-done.9, f32[3,1024]{1,0:T(4,128)S(1)} %copy-done.10, f32[3,1024]{1,0:T(4,128)S(1)} %copy-done.11, ...), kind=kLoop, calls=%fused_computation.23 | loop fusion | flops 31457280 | bytes 50421248 | tf_op jit(solution)/shard_map/add | solution.py:47
  359.1 2.8 fusion.45
  361.8 0.7 slice_bitcast_fusion
  362.6 1.7 copy.126
  364.3 1.9 reshape.397
  367.0 1.9 fusion.21
  368.9 2.7 copy.128
  371.6 3.1 reshape.394
  374.7 3.0 while.47
  374.9 0.7 bitcast_dynamic-update-slice_fusion.4
  375.7 0.7 bitcast_dynamic-update-slice_fusion.4
  376.3 0.7 bitcast_dynamic-update-slice_fusion.4
  377.0 0.7 bitcast_dynamic-update-slice_fusion.4
  377.8 0.9 slice.104
  378.7 0.8 slice.105
  379.6 0.9 slice.103
  380.5 0.8 slice.106
  381.3 1.9 collective-permute-start.1
  383.3 11.0 %all_gather.6 = f32[8,16,1024]{2,1,0:T(8,128)S(1)} all-gather(f32[1,16,1024]{2,1,0:T(8,128)S(1)} %slice.105), channel_id=1, replica_groups=mesh['ctx'=8,'ts'=4] {'ctx'}, dimensions={0}, use_global_device_ids=true | all-gather | bytes 589824 | tf_op jit(solution)/shard_map/all_gather | solution.py:23
  394.3 8.9 %all_gather.7 = f32[8,16,1024]{2,1,0:T(8,128)S(1)} all-gather(f32[1,16,1024]{2,1,0:T(8,128)S(1)} %slice.106), channel_id=1, replica_groups=mesh['ctx'=8,'ts'=4] {'ctx'}, dimensions={0}, use_global_device_ids=true | all-gather | bytes 589824 | tf_op jit(solution)/shard_map/all_gather | solution.py:23
  403.3 0.7 reshape.395
  404.0 4.6 fusion.24
  408.8 2.1 copy.131
  410.9 1.0 pad_maximum_fusion.1
  412.0 125.4 %while.46 = (s32[]{:T(128)}, f32[4,128,1024]{2,1,0:T(8,128)}, s32[4]{0:T(128)S(1)}, bf16[640,1024]{1,0:T(8,128)(2,1)S(1)}, s32[]{:T(128)}, /*index=5*/s32[1,16]{...) while((s32[]{:T(128)}, f32[4,128,1024]{2,1,0:T(8,128)}, s32[4]{0:T(128)S(1)}, ...), condition=%wide.region_6.7_spmd.clone.clone, body=%wide.region_3.6_spmd.clone.sunk.clone | while | flops 83925256 | bytes 34672892 | solution.py:161
  413.7 15.1 %convert_reduce_fusion.3 = bf16[128,256,64]{2,1,0:T(8,128)(2,1)} fusion(bf16[3,128,256,64]{3,2,1,0:T(8,128)(2,1)} %get-tuple-element.559, pred[128,256]{1,0:T(8,128)(4,1)S(1)} %broadcast_compare_fusion.5), kind=kLoop, calls=%fused_computation.5.clone.1.clone | loop fusion | flops 16777216 | bytes 16809984 | tf_op jit(solution)/shard_map/while/body/eval_jaxpr/ptug,ugc->tgc/reduce_sum | solution.py:157
  428.8 10.1 %copy.177 = bf16[128,256,64]{1,0,2:T(8,128)(2,1)} copy(bf16[128,256,64]{2,1,0:T(8,128)(2,1)} %convert_reduce_fusion.3) | data formatting | bytes 8388608 | tf_op jit(solution)/shard_map/while/body/eval_jaxpr/ptug,ugc->tgc/reduce_sum | solution.py:157
  438.9 3.4 fusion.59
  442.5 0.8 constant_dynamic-update-slice_fusion.3
  445.1 15.1 %convert_reduce_fusion.3 = bf16[128,256,64]{2,1,0:T(8,128)(2,1)} fusion(bf16[3,128,256,64]{3,2,1,0:T(8,128)(2,1)} %get-tuple-element.559, pred[128,256]{1,0:T(8,128)(4,1)S(1)} %broadcast_compare_fusion.5), kind=kLoop, calls=%fused_computation.5.clone.1.clone | loop fusion | flops 16777216 | bytes 16809984 | tf_op jit(solution)/shard_map/while/body/eval_jaxpr/ptug,ugc->tgc/reduce_sum | solution.py:157
  460.2 10.1 %copy.177 = bf16[128,256,64]{1,0,2:T(8,128)(2,1)} copy(bf16[128,256,64]{2,1,0:T(8,128)(2,1)} %convert_reduce_fusion.3) | data formatting | bytes 8388608 | tf_op jit(solution)/shard_map/while/body/eval_jaxpr/ptug,ugc->tgc/reduce_sum | solution.py:157
  470.3 3.4 fusion.59
  473.9 0.8 constant_dynamic-update-slice_fusion.3
  476.4 15.1 %convert_reduce_fusion.3 = bf16[128,256,64]{2,1,0:T(8,128)(2,1)} fusion(bf16[3,128,256,64]{3,2,1,0:T(8,128)(2,1)} %get-tuple-element.559, pred[128,256]{1,0:T(8,128)(4,1)S(1)} %broadcast_compare_fusion.5), kind=kLoop, calls=%fused_computation.5.clone.1.clone | loop fusion | flops 16777216 | bytes 16809984 | tf_op jit(solution)/shard_map/while/body/eval_jaxpr/ptug,ugc->tgc/reduce_sum | solution.py:157
  491.5 10.1 %copy.177 = bf16[128,256,64]{1,0,2:T(8,128)(2,1)} copy(bf16[128,256,64]{2,1,0:T(8,128)(2,1)} %convert_reduce_fusion.3) | data formatting | bytes 8388608 | tf_op jit(solution)/shard_map/while/body/eval_jaxpr/ptug,ugc->tgc/reduce_sum | solution.py:157
  501.6 3.4 fusion.59
  505.2 0.8 constant_dynamic-update-slice_fusion.3
  507.7 15.1 %convert_reduce_fusion.3 = bf16[128,256,64]{2,1,0:T(8,128)(2,1)} fusion(bf16[3,128,256,64]{3,2,1,0:T(8,128)(2,1)} %get-tuple-element.559, pred[128,256]{1,0:T(8,128)(4,1)S(1)} %broadcast_compare_fusion.5), kind=kLoop, calls=%fused_computation.5.clone.1.clone | loop fusion | flops 16777216 | bytes 16809984 | tf_op jit(solution)/shard_map/while/body/eval_jaxpr/ptug,ugc->tgc/reduce_sum | solution.py:157
  522.9 10.1 %copy.177 = bf16[128,256,64]{1,0,2:T(8,128)(2,1)} copy(bf16[128,256,64]{2,1,0:T(8,128)(2,1)} %convert_reduce_fusion.3) | data formatting | bytes 8388608 | tf_op jit(solution)/shard_map/while/body/eval_jaxpr/ptug,ugc->tgc/reduce_sum | solution.py:157
  532.9 3.4 fusion.59
  536.5 0.9 constant_dynamic-update-slice_fusion.3
  537.4 3.9 multiply_convert_fusion
  541.3 30.1 %all_to_all.34 = bf16[4,128,1024]{2,1,0:T(8,128)(2,1)S(1)} all-to-all(bf16[4,128,1024]{2,1,0:T(8,128)(2,1)S(1)} %multiply_convert_fusion), channel_id=1, replica_groups=mesh['ctx'=8,'ts'=4] {'ts'}, dimensions={0} | all-to-all | bytes 2097152 | tf_op jit(solution)/shard_map/all_to_all | solution.py:183
  571.5 0.7 copy.133
  572.1 1.3 copy.134
  (146 shorter events, 13.2 us)
Async XLA Ops:
  0.0 30.5 %copy-start = (f32[128,256]{1,0:T(8,128)S(1)}, f32[128,256]{1,0:T(8,128)}, u32[]{:S(2)}) copy-start(f32[128,256]{1,0:T(8,128)} %param.16) | copy-start | bytes 393220
  24.0 6.2 %copy-start.28 = (s32[16]{0:T(128)S(1)}, s32[16]{0:T(128)}, u32[]{:S(2)}) copy-start(s32[16]{0:T(128)} %param.14) | copy-start | bytes 196
  24.0 6.4 %copy-start.14 = (f32[3,7,256]{2,1,0:T(8,128)S(1)}, f32[3,7,256]{2,1,0:T(8,128)}, u32[]{:S(2)}) copy-start(f32[3,7,256]{2,1,0:T(8,128)} %param.15) | copy-start | bytes 64516
  24.0 6.8 %copy-start.15 = (f32[16,256]{1,0:T(8,128)S(1)}, f32[16,256]{1,0:T(8,128)}, u32[]{:S(2)}) copy-start(f32[16,256]{1,0:T(8,128)} %param.17) | copy-start | bytes 49156
  24.0 6.8 %copy-start.16 = (f32[16,256]{1,0:T(8,128)S(1)}, f32[16,256]{1,0:T(8,128)}, u32[]{:S(2)}) copy-start(f32[16,256]{1,0:T(8,128)} %param.18) | copy-start | bytes 49156
  24.0 282.8 %all-to-all-start = ((bf16[128,3,4096]{0,1,2:T(4,128)(2,1)}), bf16[128,3,4096]{0,1,2:T(4,128)(2,1)}, u32[]{:S(2)}, u32[]{:S(2)}) async-start(bf16[128,3,4096]{0,1,2:T(4,128)(2,1)} %copy.113), calls=%async_computation | async-start | bytes 8388608 | tf_op jit(solution)/shard_map/all_to_all | solution.py:103
  30.4 1.3 copy-start.29
  31.0 109.7 %copy-start.3 = (f32[16,64]{0,1:T(8,128)}, f32[16,64]{0,1:T(8,128)S(1)}, u32[]{:S(2)}) copy-start(f32[16,64]{0,1:T(8,128)S(1)} %copy.118) | copy-start | bytes 12292
  31.1 109.6 %copy-start.6 = (f32[16,64]{0,1:T(8,128)}, f32[16,64]{0,1:T(8,128)S(1)}, u32[]{:S(2)}) copy-start(f32[16,64]{0,1:T(8,128)S(1)} %copy.117) | copy-start | bytes 12292
  292.9 8.3 %copy-start.2 = (bf16[1,128,256,64]{2,3,1,0:T(8,128)(2,1)S(1)}, bf16[1,128,256,64]{2,3,1,0:T(8,128)(2,1)}, u32[]{:S(2)}) copy-start(bf16[1,128,256,64]{2,3,1,0:T(8,128)(2,1)} %get-tuple-element.321) | copy-start | bytes 12582916
  314.9 33.5 %collective-permute-start = (bf16[6,3,1024]{2,0,1:T(8,128)(2,1)}, bf16[6,3,1024]{2,0,1:T(8,128)(2,1)}, u32[]{:S(2)}, u32[]{:S(2)}) collective-permute-start(bf16[6,3,1024]{2,0,1:T(8,128)(2,1)} %slice.111), channel_id=1, source_target_pairs={{0,4},{4,8},{8,12},{12,16},{16,20},{20,24},{24,28},{1,5},{5,9},{9,... | collective-permute-start | bytes 110600 | tf_op jit(solution)/shard_map/ppermute | solution.py:18
  348.2 1.8 copy-start.8
  348.2 1.9 copy-start.9
  348.3 1.9 copy-start.10
  348.3 1.9 copy-start.11
  348.3 1.9 copy-start.12
  348.3 1.9 copy-start.13
  348.3 1.9 copy-start.17
  348.3 1.9 copy-start.18
  348.3 1.9 copy-start.19
  348.3 1.9 copy-start.20
  348.3 1.9 copy-start.21
  348.3 1.9 copy-start.22
  348.4 1.9 copy-start.23
  361.8 4.4 copy-start.27
  364.3 2.5 copy-start.26
  366.2 0.8 copy-start.4
  374.7 29.3 %copy-start.25 = (f32[128]{0:T(128)S(1)}, f32[128]{0:T(128)}, u32[]{:S(2)}) copy-start(f32[128]{0:T(128)} %broadcast_add_fusion) | copy-start | bytes 1540
  377.8 26.2 %copy-start.5 = (f32[16,64]{0,1:T(8,128)S(1)}, f32[16,64]{0,1:T(8,128)}, u32[]{:S(2)}) copy-start(f32[16,64]{0,1:T(8,128)} %copy-done.3) | copy-start | bytes 12292
  377.8 26.2 %copy-start.7 = (f32[16,64]{0,1:T(8,128)S(1)}, f32[16,64]{0,1:T(8,128)}, u32[]{:S(2)}) copy-start(f32[16,64]{0,1:T(8,128)} %copy-done.6) | copy-start | bytes 12292
  381.3 29.6 %collective-permute-start.1 = (bf16[128,1024]{1,0:T(8,128)(2,1)}, bf16[128,1024]{1,0:T(8,128)(2,1)}, u32[]{:S(2)}, u32[]{:S(2)}) collective-permute-start(bf16[128,1024]{1,0:T(8,128)(2,1)} %slice_bitcast_fusion), channel_id=1, source_target_pairs={{0,4},{4,8},{8,12},{12,16},{16,20},{20,24},{24,28},{1,5},{5,9},{9,... | collective-permute-start | bytes 786440 | tf_op jit(solution)/shard_map/ppermute | solution.py:18
  408.8 3.1 copy-start.30
  412.0 125.4 %dynamic-slice-start = ((f32[4096]{0:T(1024)}, s32[]{:T(128)}), f32[1024]{0:T(1024)S(1)}, s32[]{:S(2)}) async-start(f32[4096]{0:T(1024)} %param.19, s32[]{:T(128)} %select_n.139), calls=%async_computation.2 | async-start | bytes 8704 | tf_op jit(solution)/shard_map/dynamic_slice | solution.py:97
  412.0 125.4 %copy-start.24 = (pred[4,128]{1,0:T(4,128)(4,1)S(1)}, pred[4,128]{1,0:T(4,128)(4,1)}, u32[]{:S(2)}) copy-start(pred[4,128]{1,0:T(4,128)(4,1)} %broadcast_compare_fusion.2) | copy-start | bytes 1540
  537.4 36.0 %copy-start.1 = (f32[128,256]{1,0:T(8,128)S(1)}, f32[128,256]{1,0:T(8,128)}, u32[]{:S(2)}) copy-start(f32[128,256]{1,0:T(8,128)} %param.16) | copy-start | bytes 393220
where the time goes:
time: 582 us; the launch traced here: 574 us
  local copies, waits for them, and re-layouts  373 us (64%)
  other arithmetic  114 us (20%)
  blocking collectives  50 us (9%)
  matrix products  20.1 us (3%)
  starting transfers between devices  12 us (2%)
    gather x2, local copies, waits for them, and re-layouts, band_matrix(): medium_taps[lag_index] + jnp.where(same_block, long_table[lag_index], 0.0)  121 us
    gather x2, local copies, waits for them, and re-layouts, band_matrix(): long_table[lag_index]  121 us
    reduce_sum x4, other arithmetic, block_filter(): jnp.einsum('ptug,ugc->tgc', masked, window_x, preferred_element_type=jnp....  60.5 us
    reduce_sum x4, local copies, waits for them, and re-layouts, block_filter(): jnp.einsum('ptug,ugc->tgc', masked, window_x, preferred_element_type=jnp....  40.3 us
    all_to_all x1, blocking collectives, per_device(): lax.all_to_all(outgoing, 'ts', split_axis=0, concat_axis=1, tiled=True)  30.1 us
    unnamed x69, local copies, waits for them, and re-layouts  29.4 us
    reshape x1, local copies, waits for them, and re-layouts, per_device(): stacked = projected.reshape(tok_rows, 3, width)  20.5 us
    all_gather x2, blocking collectives, carried_in(): gathered = jax.tree.map(lambda a: lax.all_gather(a, axis), part)  19.9 us
  transfers between devices with their start and end apart: 3, of which 0 were waited for; matrix products, arithmetic and copies ran while one was open for 55% of the time, Pallas kernels for 0%

commit v1 on v0

v1 whole, which is shorter than its diff:
```python
import functools

import jax
import jax.numpy as jnp
from jax import lax
from jax.experimental import pallas as pl
from jax.experimental.pallas import tpu as pltpu
from jax.sharding import PartitionSpec as P

GROUP = 16
SHORT = 7
MODES = 16
LANES = 128
PER = LANES // GROUP
TILE = 512
EDGE = 8


def row_starts(lengths, begin, rows):
    position = begin + lax.broadcasted_iota(jnp.int32, (rows, LANES), 0)
    start = jnp.zeros((rows, LANES), jnp.int32)
    doc_begin = jnp.int32(0)
    for doc in range(lengths.shape[0]):
        start = jnp.where(position >= doc_begin, doc_begin, start)
        doc_begin = doc_begin + lengths[doc]
    return start, position


def short_conv(value, edge, taps, part, valid, window, lane):
    rows = value.shape[0]
    columns = pl.ds(lane * LANES, LANES)
    window[pl.ds(0, EDGE), :] = edge[:, columns].astype(jnp.float32)
    window[pl.ds(EDGE, rows), :] = value[:, columns].astype(jnp.float32)
    total = window[pl.ds(EDGE, rows), :] * taps[part, 0:1, columns]
    for offset in range(1, SHORT):
        term = window[pl.ds(EDGE - offset, rows), :] * taps[part, offset : offset + 1, columns]
        total = total + jnp.where(valid >= offset, term, 0.0)
    return total


def on_diagonal(shape):
    row = lax.broadcasted_iota(jnp.int32, shape, 0) // GROUP
    column = lax.broadcasted_iota(jnp.int32, shape, 1) // GROUP
    return row == column


def spread(block):
    lane_group = lax.broadcasted_iota(jnp.int32, (1, LANES), 1) // GROUP
    parts = [jnp.where(lane_group == g, block, 0.0) for g in range(PER)]
    return jnp.concatenate(parts, axis=0).astype(jnp.bfloat16)


def circulants(rows_ref, lane, mask, band):
    for g in range(PER):
        taps = rows_ref[pl.ds(lane * PER + g, 1), :]
        wheel = pltpu.roll(
            jnp.broadcast_to(taps, (LANES, LANES)), 0, 1, stride=1, stride_axis=0
        )
        band[:, pl.ds(g * LANES, LANES)] = jnp.where(mask, wheel, 0.0).astype(jnp.bfloat16)


def product_kernel(lengths, begin, k_ref, v_ref, ke_ref, ve_ref, taps, tail, out, state, window):
    rows = k_ref.shape[0]
    start, position = row_starts(lengths, begin[0], rows)
    valid = position - start
    last = jnp.max(start)
    diagonal = on_diagonal((LANES, LANES))
    for lane in range(TILE // LANES):
        columns = pl.ds(lane * LANES, LANES)
        key = short_conv(k_ref, ke_ref, taps, 1, valid, window.at[0], lane)
        value = short_conv(v_ref, ve_ref, taps, 2, valid, window.at[1], lane)
        product = (key * value).astype(jnp.bfloat16)
        out[:, columns] = product
        kept = jnp.where(position >= last, product.astype(jnp.float32), 0.0).astype(jnp.bfloat16)
        full = jnp.dot(tail[columns, :], kept, preferred_element_type=jnp.float32)
        full = jnp.where(diagonal, full, 0.0)
        summed = full[0:MODES]
        for g in range(1, PER):
            summed = summed + full[g * MODES : (g + 1) * MODES]
        state[:, columns] = summed


def local_kernel(
    lengths, begin, x_ref, q_ref, qe_ref, taps, wheel, skip, partial, query, window, band
):
    rows = x_ref.shape[0]
    start, position = row_starts(lengths, begin[0], rows)
    valid = position - start
    row = lax.broadcasted_iota(jnp.int32, (rows, LANES), 0)
    column = lax.broadcasted_iota(jnp.int32, (rows, LANES), 1)
    mask = (column <= row) & (column + begin[0] >= start)
    for lane in range(TILE // LANES):
        columns = pl.ds(lane * LANES, LANES)
        query[:, columns] = short_conv(q_ref, qe_ref, taps, 0, valid, window, lane)
        block = x_ref[:, columns].astype(jnp.float32)
        circulants(wheel, lane, mask, band.at[lane % 2])
        summed = jnp.dot(band[lane % 2], spread(block), preferred_element_type=jnp.float32)
        partial[:, columns] = summed + skip[:, columns] * block


def final_kernel(
    lengths, begin, x_ref, wheel, decay, state, partial, query, out, band
):
    rows = x_ref.shape[0]
    start, position = row_starts(lengths, begin[0], rows)
    row = lax.broadcasted_iota(jnp.int32, (rows, LANES), 0)
    column = lax.broadcasted_iota(jnp.int32, (rows, LANES), 1)
    mask = (column > row) & (column + (begin[0] - rows) >= start)
    carried_rows = start < begin[0]
    diagonal = on_diagonal((LANES, LANES))
    for lane in range(TILE // LANES):
        columns = pl.ds(lane * LANES, LANES)
        block = x_ref[:, columns].astype(jnp.float32)
        circulants(wheel, lane, mask, band.at[lane % 2])
        summed = jnp.dot(band[lane % 2], spread(block), preferred_element_type=jnp.float32)
        stacked = jnp.concatenate([state[:, columns]] * PER, axis=0)
        stacked = jnp.where(diagonal, stacked, 0.0).astype(jnp.bfloat16)
        carried = jnp.dot(decay[:, columns], stacked, preferred_element_type=jnp.float32)
        carried = jnp.where(carried_rows, carried, 0.0)
        filtered = (partial[:, columns] + summed + carried).astype(jnp.bfloat16)
        out[:, columns] = (query[:, columns] * filtered.astype(jnp.float32)).astype(jnp.bfloat16)


def block(shape, index):
    return pl.BlockSpec(shape, index)


def per_device(projected, doc_lengths, short_taps, medium_taps, decay_rates, residues, skip_gain):
    ts_count, ctx_count = lax.axis_size("ts"), lax.axis_size("ctx")
    ts_index, ctx_index = lax.axis_index("ts"), lax.axis_index("ctx")
    rows, width = projected.shape[0], projected.shape[1] // 3
    total = rows * ts_count * ctx_count
    span = rows * ts_count
    reach = -(-(total // 4) // span)
    devices = ts_count * ctx_count
    pairs = [(i, i + 1) for i in range(devices - 1)]
    everyone = ("ctx", "ts")
    tiles = width // TILE
    groups_tile = TILE // GROUP

    edge_kv = lax.ppermute(projected[rows - EDGE :, width:], everyone, pairs)
    edge_q = lax.ppermute(projected[rows - EDGE :, :width], everyone, pairs)

    begin = (ctx_index * ts_count + ts_index) * rows
    begin_array = jnp.full((1,), begin, jnp.int32)
    steps = jnp.arange(rows, dtype=jnp.float32)
    back = (rows - jnp.arange(rows)) % rows
    back_f = back.astype(jnp.float32)
    scaled = residues * jnp.sqrt(-jnp.expm1(-2.0 * decay_rates))
    medium_rows = jnp.concatenate([medium_taps[:1], medium_taps[:0:-1]], axis=0).T
    long_rows = jnp.sum(
        scaled[:, :, None] * jnp.exp(-decay_rates[:, :, None] * back_f[None, None]), axis=0
    )
    own_rows = medium_rows + long_rows
    rates_flat = decay_rates.T.reshape(-1)
    scaled_flat = scaled.T.reshape(-1)
    tail = jnp.exp(-rates_flat[:, None] * (rows - 1.0 - steps)[None, :]).astype(jnp.bfloat16)
    decay = (scaled_flat[None] * jnp.exp(-rates_flat[None] * (steps + 1.0)[:, None])).astype(
        jnp.bfloat16
    )
    taps = jnp.repeat(short_taps, GROUP, axis=2)
    rates_wide = jnp.repeat(decay_rates, GROUP, axis=1)

    smem = pl.BlockSpec(memory_space=pltpu.SMEM)
    tile = lambda part=0: block((rows, TILE), lambda i: (0, i + part * tiles))
    edge = lambda part=0: block((EDGE, TILE), lambda i: (0, i + part * tiles))
    taps_tile = block((3, SHORT, TILE), lambda i: (0, 0, i))
    state_tile = block((MODES, TILE), lambda i: (0, i))
    wheel_tile = block((groups_tile, rows), lambda i: (i, 0))
    wide = lambda dtype: jax.ShapeDtypeStruct((rows, width), dtype)
    product, state = pl.pallas_call(
        product_kernel,
        grid=(tiles,),
        in_specs=[smem, smem, tile(1), tile(2), edge(0), edge(1), taps_tile,
                  block((TILE, rows), lambda i: (i, 0))],
        out_specs=[tile(), state_tile],
        out_shape=[wide(jnp.bfloat16), jax.ShapeDtypeStruct((MODES, width), jnp.float32)],
        scratch_shapes=[pltpu.VMEM((2, EDGE + rows, LANES), jnp.float32)],
        name="product",
    )(doc_lengths, begin_array, projected, projected, edge_kv, edge_kv, taps, tail)

    before = lax.ppermute(product, everyone, pairs)

    ends = jnp.cumsum(doc_lengths)
    begins = ends - doc_lengths

    def start_of(position):
        return jnp.max(jnp.where(begins <= position, begins, 0))

    def faded(distance, alive):
        return jnp.where(alive, jnp.exp(-rates_wide * (distance * jnp.float32(rows))), 0.0)

    last_own = start_of(begin + rows - 1)
    last_before = start_of(jnp.maximum(begin - 1, 0))
    span_begin = ctx_index * span
    last_span = start_of(span_begin + span - 1)
    to_end = (ts_count - 1 - ts_index).astype(jnp.float32)
    step_in = faded(1.0, last_own < begin)
    running, entered = state, jnp.zeros_like(state)
    rest = state * faded(to_end, last_span <= begin + rows - 1)
    for hop in range(ts_count - 1):
        got = lax.ppermute(running.astype(jnp.bfloat16), "ts", [(hop, hop + 1)])
        back_hop = ts_count - 1 - hop
        got_rest = lax.ppermute(rest.astype(jnp.bfloat16), "ts", [(back_hop, back_hop - 1)])
        got = got.astype(jnp.float32)
        entered = entered + got
        running = running + step_in * got
        rest = rest + got_rest.astype(jnp.float32)
    whole = rest + faded(to_end + 1.0, last_span < begin) * entered
    whole = whole.astype(jnp.bfloat16)
    for hop in range(1, reach + 1):
        if hop >= ctx_count:
            break
        got = lax.ppermute(whole, "ctx", [(i, i + hop) for i in range(ctx_count - hop)])
        distance = (ts_index + (hop - 1) * ts_count).astype(jnp.float32)
        alive = last_before <= span_begin - (hop - 1) * span - 1
        entered = entered + faded(distance, alive) * got.astype(jnp.float32)

    partial, query = pl.pallas_call(
        local_kernel,
        grid=(tiles,),
        in_specs=[smem, smem, tile(), tile(), edge(), taps_tile, wheel_tile,
                  block((1, TILE), lambda i: (0, i))],
        out_specs=[tile(), tile()],
        out_shape=[wide(jnp.float32), wide(jnp.float32)],
        scratch_shapes=[
            pltpu.VMEM((EDGE + rows, LANES), jnp.float32),
            pltpu.VMEM((2, rows, PER * LANES), jnp.bfloat16),
        ],
        cost_estimate=pl.CostEstimate(
            flops=2 * rows * rows * width * PER, bytes_accessed=rows * width * 12, transcendentals=0
        ),
        name="local",
    )(doc_lengths, begin_array, product, projected, edge_q, taps, own_rows, skip_gain[None])

    return pl.pallas_call(
        final_kernel,
        grid=(tiles,),
        in_specs=[smem, smem, tile(), wheel_tile, tile(), state_tile, tile(), tile()],
        out_specs=tile(),
        out_shape=wide(jnp.bfloat16),
        scratch_shapes=[pltpu.VMEM((2, rows, PER * LANES), jnp.bfloat16)],
        name="final",
    )(doc_lengths, begin_array, before, medium_rows, decay, entered, partial, query)


def solution(mesh):
    return jax.shard_map(
        per_device,
        mesh=mesh,
        in_specs=(P(("ctx", "ts"), None), P(), P(), P(), P(), P(), P()),
        out_specs=P(("ctx", "ts"), None),
        check_vma=False,
    )
```

time: 582 us -> 97.1 us (0.17); the launches traced: 574 us -> 95.9 us
  local copies, waits for them, and re-layouts: 373 us -> 20.9 us
  other arithmetic: 114 us -> 12 us
  blocking collectives: 50 us -> 0 us
  Pallas kernels: 0 us -> 27.4 us
  matrix products: 20.1 us -> 0 us
  starting transfers between devices: 12 us -> 30.2 us
    gather x4 -> x0, local copies, waits for them, and re-layouts: 242 us -> none  [the longest x2 121 us: band_matrix(): medium_taps[lag_index] + jnp.where(same_block, long_table[lag_index], 0.0)]
    reduce_sum x5 -> x1, other arithmetic: 60.8 us -> 1.97 us  [per_device(): jnp.sum(scaled[:, :, None] * jnp.exp(-decay_rates[:, :, None] * back_f[No...]
    reduce_sum x5 -> x0, local copies, waits for them, and re-layouts: 40.4 us -> none  [the longest x4 40.3 us: block_filter(): jnp.einsum('ptug,ugc->tgc', masked, window_x, preferred_element_type=jnp....]
    all_to_all x1 -> x0, blocking collectives: 30.1 us -> none  [per_device(): lax.all_to_all(outgoing, 'ts', split_axis=0, concat_axis=1, tiled=True)]
    unnamed x69 -> x13, local copies, waits for them, and re-layouts: 29.4 us -> 0.77 us
    pallas_call x0 -> x3, Pallas kernels: none -> 27.4 us  [the longest x1 9.56 us: per_device(): pl.pallas_call(local_kernel, grid=(tiles,), in_specs=[smem, smem, tile(),...]
    reshape x6 -> x1, local copies, waits for them, and re-layouts: 29.9 us -> 2.5 us  [per_device(): taps = jnp.repeat(short_taps, GROUP, axis=2)]
    convert_element_type x6 -> x9, other arithmetic: 30.4 us -> 5.49 us  [the longest x1 1.51 us: per_device(): jnp.exp(-rates_flat[:, None] * (rows - 1.0 - steps)[None, :])]
  transfers between devices with their start and end apart: 3 -> 11, of which waited for: 0 -> 1; matrix products, arithmetic and copies ran while one was open for 55% -> 31% of each run, Pallas kernels for 0% -> 10%
where the time goes in v1:
time: 97.1 us; the launch traced here: 95.9 us
  starting transfers between devices  30.2 us (31%)
  Pallas kernels  27.4 us (28%)
  local copies, waits for them, and re-layouts  20.9 us (22%)
  other arithmetic  12 us (12%)
  between operations  3.47 us (4%)
  waiting for transfers between devices  1.88 us (2%)
    ppermute x2, starting transfers between devices, per_device(): lax.ppermute(whole, 'ctx', [(i, i + hop) for i in range(ctx_count - hop)])  9.92 us
    pallas_call x1, Pallas kernels, per_device(): pl.pallas_call(local_kernel, grid=(tiles,), in_specs=[smem, smem, tile(),...  9.56 us
    pallas_call x1, Pallas kernels, per_device(): pl.pallas_call(final_kernel, grid=(tiles,), in_specs=[smem, smem, tile(),...  9.08 us
    pallas_call x1, Pallas kernels, per_device(): pl.pallas_call(product_kernel, grid=(tiles,), in_specs=[smem, smem, tile(...  8.79 us
    select_n x5, local copies, waits for them, and re-layouts, faded(): jnp.where(alive, jnp.exp(-rates_wide * (distance * jnp.float32(rows))), 0.0)  7.79 us
    ppermute x1, starting transfers between devices, per_device(): before = lax.ppermute(product, everyone, pairs)  4.96 us
    ppermute x3, starting transfers between devices, per_device(): got = lax.ppermute(running.astype(jnp.bfloat16), 'ts', [(hop, hop + 1)])  4.55 us
    ppermute x1, starting transfers between devices, per_device(): edge_q = lax.ppermute(projected[rows - EDGE:, :width], everyone, pairs)  4.14 us
  transfers between devices with their start and end apart: 11, of which 1 were waited for; matrix products, arithmetic and copies ran while one was open for 31% of the time, Pallas kernels for 10%

profile of v1, /device:TPU:1, one launch (start us, length us, event | category | flops | bytes accessed | tf_op | source)
XLA Modules:
  0.0 95.9 jit_solution(7547431161653992517)
XLA Ops:
  0.0 0.9 slice.12
  0.9 4.0 %collective-permute-start = (bf16[8,8192]{1,0:T(8,128)(2,1)S(1)}, bf16[8,8192]{1,0:T(8,128)(2,1)S(1)}, u32[]{:S(2)}, u32[]{:S(2)}) collective-permute-start(bf16[8,8192]{1,0:T(8,128)(2,1)S(1)} %slice.12), channel_id=1, source_target_pairs={{0,1},{1,2},{2,3},{3,4},{4,5},{5,6},{6,7},{7,8},{8,9},{9,10},{10,1... | collective-permute-start | bytes 393224 | tf_op jit(solution)/shard_map/ppermute | solution.py:141
  5.0 0.7 copy.20
  5.7 0.1 reduce
  5.9 1.4 %fusion.9 = (s32[]{:T(128)}, s32[]{:T(128)}, s32[]{:T(128)}) fusion(s32[]{:T(128)S(6)} %sub.46, s32[16]{0:T(128)S(1)} %reduce, s32[16]{0:T(128)} %lengths.5, s32[]{:T(128)S(6)} %sub.49, s32[]{:T(128)S(6)} %max.3), kind=kLoop, calls=%fused_computation.32 | loop fusion | flops 157 | bytes 152 | tf_op jit(solution)/shard_map/reduce_max | solution.py:188
  10.4 1.4 %exponential_select_fusion.3 = (f32[16,256]{1,0:T(8,128)}, f32[256,16]{0,1:T(8,128)S(1)}, f32[16,256]{1,0:T(8,128)S(1)}, f32[16,256]{1,0:T(8,128)S(1)}, f32[16,2...) fusion(f32[]{:T(128)S(6)} %mul.164, pred[]{:T(512)S(6)} %le.31, f32[16,256]{1,0:T(8,128)} %param.11, ...), kind=kLoop, calls=%fused_computation.21 | loop fusion | flops 57344 | bytes 163861 | tf_op jit(solution)/shard_map/jit(_where)/select_n | solution.py:191
  11.8 0.1 copy.16
  11.9 0.1 neg.34
  12.0 1.5 %exponential_convert_fusion.tail = bf16[4096,128]{1,0:T(8,128)(2,1)} fusion(f32[128]{0:T(128)S(1)} %iota_subtract_fusion, f32[4096]{0:T(1024)S(1)} %neg.34), kind=kLoop, calls=%fused_computation.2 | loop fusion | flops 1048576 | bytes 1065472 | tf_op jit(solution)/shard_map/convert_element_type | solution.py:157
  13.5 1.5 %broadcast_in_dim.40 = f32[3,7,256,16]{3,2,1,0:T(8,128)S(1)} broadcast(f32[3,7,256]{2,1,0:T(8,128)} %param.9), dimensions={0,1,2} | broadcast | bytes 365568 | tf_op jit(solution)/shard_map/broadcast_in_dim | solution.py:161
  15.0 2.5 %reshape.104.taps = f32[3,7,4096]{2,1,0:T(8,128)} reshape(f32[3,7,256,16]{3,2,1,0:T(8,128)S(1)} %broadcast_in_dim.40) | data formatting | bytes 688128 | tf_op jit(solution)/shard_map/reshape | solution.py:161
  17.5 0.0 collective-permute-done.ke_ref.ve_ref
  17.5 0.7 copy-done.1
  18.2 8.8 %product.1 = (bf16[128,4096]{1,0:T(8,128)(2,1)}, f32[16,4096]{1,0:T(8,128)}) custom-call(s32[16]{0:T(128)} %lengths.5, s32[1]{0:T(128)} %bitcast.begin, bf16[128,12288]{1,0:T(8,128)(2,1)} %q_ref.1, bf16[128,12288]{1,0:T(8,128)(2,1)} %q_ref.1, bf16[8,8192]{1,0:T(8,128)(2,1)} %copy-done.1, bf16[8,8192]{1,0:T(8,128)(2,1)} %copy-done.1, ...), custom_call_target="tpu_custom_call" | custom-call | tf_op jit(solution)/shard_map/product/pallas_call | solution.py:171
  27.0 1.0 %convert_element_type.69 = bf16[16,4096]{1,0:T(8,128)(2,1)S(1)} convert(f32[16,4096]{1,0:T(8,128)} %get-tuple-element.10) | non-fusion elementwise | flops 65536 | bytes 393216 | tf_op jit(solution)/shard_map/convert_element_type | solution.py:202
  27.9 3.2 %collective-permute-start.2 = (bf16[16,4096]{1,0:T(8,128)(2,1)S(1)}, bf16[16,4096]{1,0:T(8,128)(2,1)S(1)}, u32[]{:S(2)}, u32[]{:S(2)}) collective-permute-start(bf16[16,4096]{1,0:T(8,128)(2,1)S(1)} %convert_element_type.69), channel_id=1, source_target_pairs={{0,1},{4,5},{8,9},{12,13},{16,17},{20,21},{24,25},{28,29}} | collective-permute-start | bytes 393224 | tf_op jit(solution)/shard_map/ppermute | solution.py:202
  31.2 0.6 broadcast_in_dim.43
  31.8 1.6 %select_n.76 = f32[16,4096]{1,0:T(8,128)S(1)} reshape(f32[16,256,16]{2,1,0:T(8,128)S(1)} %broadcast_in_dim.43) | data formatting | bytes 524288 | tf_op jit(solution)/shard_map/jit(_where)/select_n | solution.py:191
  33.3 0.0 collective-permute-done.2
  33.3 0.0 copy-done
  33.4 0.7 collective-permute-start.3
  34.1 0.6 broadcast_in_dim.45
  34.7 1.6 %select_n.84 = f32[16,4096]{1,0:T(8,128)S(1)} reshape(f32[16,256,16]{2,1,0:T(8,128)S(1)} %broadcast_in_dim.45) | data formatting | bytes 524288 | tf_op jit(solution)/shard_map/jit(_where)/select_n | solution.py:191
  36.2 0.0 collective-permute-done.3
  36.2 0.7 fusion.13
  37.0 0.7 collective-permute-start.5
  37.6 1.5 %slice.15 = bf16[8,4096]{1,0:T(8,128)(2,1)} slice(bf16[128,12288]{1,0:T(8,128)(2,1)} %q_ref.1), slice={[120:128], [0:4096]} | slice | bytes 131072 | tf_op jit(solution)/shard_map/slice | solution.py:142
  39.1 4.1 %collective-permute-start.10 = (bf16[8,4096]{1,0:T(8,128)(2,1)}, bf16[8,4096]{1,0:T(8,128)(2,1)}, u32[]{:S(2)}, u32[]{:S(2)}) collective-permute-start(bf16[8,4096]{1,0:T(8,128)(2,1)} %slice.15), channel_id=1, source_target_pairs={{0,1},{1,2},{2,3},{3,4},{4,5},{5,6},{6,7},{7,8},{8,9},{9,10},{10,1... | collective-permute-start | bytes 196616 | tf_op jit(solution)/shard_map/ppermute | solution.py:142
  43.2 0.8 copy.19
  44.1 0.1 mul.153
  44.2 0.0 collective-permute-done.5
  44.2 0.7 fusion.4
  44.9 0.7 collective-permute-start.6
  45.5 1.4 %multiply_convert_fusion.decay = bf16[128,4096]{1,0:T(8,128)(2,1)} fusion(f32[128]{0:T(128)S(1)} %iota_add_fusion, f32[4096]{0:T(1024)S(1)} %neg.34, f32[4096]{0:T(1024)S(1)} %mul.153), kind=kLoop, calls=%fused_computation.1 | loop fusion | flops 1572864 | bytes 1081856 | tf_op jit(solution)/shard_map/convert_element_type | solution.py:158
  46.9 0.0 slice-start
  47.0 0.0 copy-start.3
  47.0 1.3 %broadcast_in_dim.46 = f32[16,256,16]{2,1,0:T(8,128)S(1)} broadcast(f32[16,256]{1,0:T(8,128)} %get-tuple-element.25), dimensions={0,1} | broadcast | bytes 278528 | tf_op jit(solution)/shard_map/broadcast_in_dim | solution.py:162
  48.3 1.6 %select_n.87 = f32[16,4096]{1,0:T(8,128)S(1)} reshape(f32[16,256,16]{2,1,0:T(8,128)S(1)} %broadcast_in_dim.46) | data formatting | bytes 524288 | tf_op jit(solution)/shard_map/jit(_where)/select_n | solution.py:191
  49.9 0.1 copy.21
  50.0 0.2 rev.3
  50.2 0.0 slice-done
  50.2 0.1 copy.18
  50.4 0.7 collective-permute-start.4
  51.0 0.0 collective-permute-done.6
  51.1 1.3 %collective-permute-start.7 = (bf16[16,4096]{1,0:T(8,128)(2,1)S(1)}, bf16[16,4096]{1,0:T(8,128)(2,1)S(1)}, u32[]{:S(2)}, u32[]{:S(2)}) collective-permute-start(bf16[16,4096]{1,0:T(8,128)(2,1)S(1)} %fusion.5), channel_id=1, source_target_pairs={{1,0},{5,4},{9,8},{13,12},{17,16},{21,20},{25,24},{29,28}} | collective-permute-start | bytes 393224 | tf_op jit(solution)/shard_map/ppermute | solution.py:204
  52.4 2.0 %multiply_reduce_fusion = f32[256,128]{1,0:T(8,128)S(1)} fusion(f32[128]{0:T(128)S(1)} %fusion.7, f32[16,256]{1,0:T(8,128)} %get-tuple-element.28, f32[16,256]{1,0:T(8,128)} %get-tuple-element.27), kind=kLoop, calls=%fused_computation | loop fusion | flops 1540096 | bytes 164352 | tf_op jit(solution)/shard_map/reduce_sum | solution.py:151
  54.4 5.0 %collective-permute-start.1 = (bf16[128,4096]{1,0:T(8,128)(2,1)}, bf16[128,4096]{1,0:T(8,128)(2,1)}, u32[]{:S(2)}, u32[]{:S(2)}) collective-permute-start(bf16[128,4096]{1,0:T(8,128)(2,1)} %get-tuple-element.9.x_ref), channel_id=1, source_target_pairs={{0,1},{1,2},{2,3},{3,4},{4,5},{5,6},{6,7},{7,8},{8,9},{9,10},{10,1... | collective-permute-start | bytes 3145736 | tf_op jit(solution)/shard_map/ppermute | solution.py:182
  59.3 0.0 collective-permute-done.4
  59.4 0.0 collective-permute-done.7
  59.4 0.1 add_convert_fusion
  59.5 6.8 %collective-permute-start.8 = (bf16[16,4096]{1,0:T(8,128)(2,1)S(1)}, bf16[16,4096]{1,0:T(8,128)(2,1)S(1)}, u32[]{:S(2)}, u32[]{:S(2)}) collective-permute-start(bf16[16,4096]{1,0:T(8,128)(2,1)S(1)} %add_convert_fusion), channel_id=1, source_target_pairs={{0,4},{4,8},{8,12},{12,16},{16,20},{20,24},{24,28},{1,5},{5,9},{9,... | collective-permute-start | bytes 393224 | tf_op jit(solution)/shard_map/ppermute | solution.py:214
  66.3 3.1 %collective-permute-start.9 = (bf16[16,4096]{1,0:T(8,128)(2,1)S(1)}, bf16[16,4096]{1,0:T(8,128)(2,1)S(1)}, u32[]{:S(2)}, u32[]{:S(2)}) collective-permute-start(bf16[16,4096]{1,0:T(8,128)(2,1)S(1)} %add_convert_fusion), channel_id=1, source_target_pairs={{0,8},{4,12},{8,16},{12,20},{16,24},{20,28},{1,9},{5,13},{9,17},{1... | collective-permute-start | bytes 393224 | tf_op jit(solution)/shard_map/ppermute | solution.py:214
  69.4 0.8 fusion.12
  70.2 0.6 broadcast_in_dim.44
  70.8 1.6 %select_n.80 = f32[16,4096]{1,0:T(8,128)S(1)} reshape(f32[16,256,16]{2,1,0:T(8,128)S(1)} %broadcast_in_dim.44) | data formatting | bytes 524288 | tf_op jit(solution)/shard_map/jit(_where)/select_n | solution.py:191
  72.4 0.6 broadcast_in_dim.47
  73.0 1.6 %select_n.90 = f32[16,4096]{1,0:T(8,128)S(1)} reshape(f32[16,256,16]{2,1,0:T(8,128)S(1)} %broadcast_in_dim.47) | data formatting | bytes 524288 | tf_op jit(solution)/shard_map/jit(_where)/select_n | solution.py:191
  74.6 0.0 collective-permute-done.10.qe_ref
  74.6 9.6 %local.1 = (f32[128,4096]{1,0:T(8,128)}, f32[128,4096]{1,0:T(8,128)}) custom-call(s32[16]{0:T(128)} %lengths.5, s32[1]{0:T(128)} %bitcast.begin, bf16[128,4096]{1,0:T(8,128)(2,1)} %get-tuple-element.9.x_ref, bf16[128,12288]{1,0:T(8,128)(2,1)} %q_ref.1, bf16[8,4096]{1,0:T(8,128)(2,1)} %collective-permute-done.10.qe_ref, f32[3,7,4096]{2,1,0:T(8,128)} %reshape.104.taps, ...), custom_call_target="tpu_custom_call" | custom-call | flops 1073741824 | bytes 6291456 | tf_op jit(solution)/shard_map/local/pallas_call | solution.py:219
  84.1 0.0 collective-permute-done.8
  84.1 0.0 collective-permute-done.9
  84.1 0.8 multiply_add_fusion.state
  84.9 1.9 %collective-permute-done.1.x_ref = bf16[128,4096]{1,0:T(8,128)(2,1)} collective-permute-done((bf16[128,4096]{1,0:T(8,128)(2,1)}, bf16[128,4096]{1,0:T(8,128)(2,1)}, u32[]{:S(2)}, u32[]{:S(2)}) %collective-permute-start.1) | collective-permute-done | bytes 1048608 | tf_op jit(solution)/shard_map/ppermute | solution.py:182
  86.8 9.1 %final.1 = bf16[128,4096]{1,0:T(8,128)(2,1)} custom-call(s32[16]{0:T(128)} %lengths.5, s32[1]{0:T(128)} %bitcast.begin, bf16[128,4096]{1,0:T(8,128)(2,1)} %collective-permute-done.1.x_ref, f32[256,128]{1,0:T(8,128)} %get-tuple-element.17.wheel, bf16[128,4096]{1,0:T(8,128)(2,1)} %multiply_convert_fusion.decay, f32[16,4096]{1,0:T(8,128)} %multiply_add_fusion.state, ...), custom_call_target="tpu_custom_call" | custom-call | tf_op jit(solution)/shard_map/final/pallas_call | solution.py:236
  (16 shorter events, 0.2 us)
Async XLA Ops:
  0.9 16.6 %collective-permute-start = (bf16[8,8192]{1,0:T(8,128)(2,1)S(1)}, bf16[8,8192]{1,0:T(8,128)(2,1)S(1)}, u32[]{:S(2)}, u32[]{:S(2)}) collective-permute-start(bf16[8,8192]{1,0:T(8,128)(2,1)S(1)} %slice.12), channel_id=1, source_target_pairs={{0,1},{1,2},{2,3},{3,4},{4,5},{5,6},{6,7},{7,8},{8,9},{9,10},{10,1... | collective-permute-start | bytes 393224 | tf_op jit(solution)/shard_map/ppermute | solution.py:141
  17.5 0.7 copy-start.1
  27.9 5.4 %collective-permute-start.2 = (bf16[16,4096]{1,0:T(8,128)(2,1)S(1)}, bf16[16,4096]{1,0:T(8,128)(2,1)S(1)}, u32[]{:S(2)}, u32[]{:S(2)}) collective-permute-start(bf16[16,4096]{1,0:T(8,128)(2,1)S(1)} %convert_element_type.69), channel_id=1, source_target_pairs={{0,1},{4,5},{8,9},{12,13},{16,17},{20,21},{24,25},{28,29}} | collective-permute-start | bytes 393224 | tf_op jit(solution)/shard_map/ppermute | solution.py:202
  31.2 2.2 %copy-start = (f32[16,4096]{1,0:T(8,128)S(1)}, f32[16,4096]{1,0:T(8,128)}, u32[]{:S(2)}) copy-start(f32[16,4096]{1,0:T(8,128)} %get-tuple-element.10) | copy-start | bytes 786436
  33.4 2.8 %collective-permute-start.3 = (bf16[16,4096]{1,0:T(8,128)(2,1)S(1)}, bf16[16,4096]{1,0:T(8,128)(2,1)S(1)}, u32[]{:S(2)}, u32[]{:S(2)}) collective-permute-start(bf16[16,4096]{1,0:T(8,128)(2,1)S(1)} %fusion.6), channel_id=1, source_target_pairs={{1,2},{5,6},{9,10},{13,14},{17,18},{21,22},{25,26},{29,30}} | collective-permute-start | bytes 393224 | tf_op jit(solution)/shard_map/ppermute | solution.py:202
  36.2 10.7 %copy-start.2 = (f32[128,256]{1,0:T(8,128)S(1)}, f32[128,256]{1,0:T(8,128)}, u32[]{:S(2)}) copy-start(f32[128,256]{1,0:T(8,128)} %param.10) | copy-start | bytes 393220
  37.0 7.2 %collective-permute-start.5 = (bf16[16,4096]{1,0:T(8,128)(2,1)S(1)}, bf16[16,4096]{1,0:T(8,128)(2,1)S(1)}, u32[]{:S(2)}, u32[]{:S(2)}) collective-permute-start(bf16[16,4096]{1,0:T(8,128)(2,1)S(1)} %get-tuple-element.18), channel_id=1, source_target_pairs={{3,2},{7,6},{11,10},{15,14},{19,18},{23,22},{27,26},{31,30}} | collective-permute-start | bytes 393224 | tf_op jit(solution)/shard_map/ppermute | solution.py:204
  39.1 35.5 %collective-permute-start.10 = (bf16[8,4096]{1,0:T(8,128)(2,1)}, bf16[8,4096]{1,0:T(8,128)(2,1)}, u32[]{:S(2)}, u32[]{:S(2)}) collective-permute-start(bf16[8,4096]{1,0:T(8,128)(2,1)} %slice.15), channel_id=1, source_target_pairs={{0,1},{1,2},{2,3},{3,4},{4,5},{5,6},{6,7},{7,8},{8,9},{9,10},{10,1... | collective-permute-start | bytes 196616 | tf_op jit(solution)/shard_map/ppermute | solution.py:142
  44.9 6.2 %collective-permute-start.6 = (bf16[16,4096]{1,0:T(8,128)(2,1)}, bf16[16,4096]{1,0:T(8,128)(2,1)S(1)}, u32[]{:S(2)}, u32[]{:S(2)}) collective-permute-start(bf16[16,4096]{1,0:T(8,128)(2,1)} %fusion.4), channel_id=1, source_target_pairs={{2,1},{6,5},{10,9},{14,13},{18,17},{22,21},{26,25},{30,29}} | collective-permute-start | bytes 393224 | tf_op jit(solution)/shard_map/ppermute | solution.py:204
  46.9 3.2 %slice-start = ((f32[128,256]{1,0:T(8,128)}), f32[1,256]{1,0:T(1,128)S(1)}, s32[]{:S(2)}) async-start(f32[128,256]{1,0:T(8,128)} %param.10), calls=%async_computation | async-start | bytes 2048 | tf_op jit(solution)/shard_map/slice | solution.py:150
  47.0 3.4 %copy-start.3 = (bf16[16,4096]{1,0:T(8,128)(2,1)S(1)}, bf16[16,4096]{1,0:T(8,128)(2,1)}, u32[]{:S(2)}) copy-start(bf16[16,4096]{1,0:T(8,128)(2,1)} %get-tuple-element.20) | copy-start | bytes 393220
  50.0 20.3 %copy-start.5 = (f32[16,256]{1,0:T(8,128)S(1)}, f32[16,256]{1,0:T(8,128)}, u32[]{:S(2)}) copy-start(f32[16,256]{1,0:T(8,128)} %get-tuple-element.21) | copy-start | bytes 49156
  50.4 9.0 %collective-permute-start.4 = (bf16[16,4096]{1,0:T(8,128)(2,1)S(1)}, bf16[16,4096]{1,0:T(8,128)(2,1)S(1)}, u32[]{:S(2)}, u32[]{:S(2)}) collective-permute-start(bf16[16,4096]{1,0:T(8,128)(2,1)S(1)} %copy-done.3), channel_id=1, source_target_pairs={{2,3},{6,7},{10,11},{14,15},{18,19},{22,23},{26,27},{30,31}} | collective-permute-start | bytes 393224 | tf_op jit(solution)/shard_map/ppermute | solution.py:202
  51.1 8.3 %collective-permute-start.7 = (bf16[16,4096]{1,0:T(8,128)(2,1)S(1)}, bf16[16,4096]{1,0:T(8,128)(2,1)S(1)}, u32[]{:S(2)}, u32[]{:S(2)}) collective-permute-start(bf16[16,4096]{1,0:T(8,128)(2,1)S(1)} %fusion.5), channel_id=1, source_target_pairs={{1,0},{5,4},{9,8},{13,12},{17,16},{21,20},{25,24},{29,28}} | collective-permute-start | bytes 393224 | tf_op jit(solution)/shard_map/ppermute | solution.py:204
  54.4 32.4 %collective-permute-start.1 = (bf16[128,4096]{1,0:T(8,128)(2,1)}, bf16[128,4096]{1,0:T(8,128)(2,1)}, u32[]{:S(2)}, u32[]{:S(2)}) collective-permute-start(bf16[128,4096]{1,0:T(8,128)(2,1)} %get-tuple-element.9.x_ref), channel_id=1, source_target_pairs={{0,1},{1,2},{2,3},{3,4},{4,5},{5,6},{6,7},{7,8},{8,9},{9,10},{10,1... | collective-permute-start | bytes 3145736 | tf_op jit(solution)/shard_map/ppermute | solution.py:182
  59.5 24.6 %collective-permute-start.8 = (bf16[16,4096]{1,0:T(8,128)(2,1)S(1)}, bf16[16,4096]{1,0:T(8,128)(2,1)S(1)}, u32[]{:S(2)}, u32[]{:S(2)}) collective-permute-start(bf16[16,4096]{1,0:T(8,128)(2,1)S(1)} %add_convert_fusion), channel_id=1, source_target_pairs={{0,4},{4,8},{8,12},{12,16},{16,20},{20,24},{24,28},{1,5},{5,9},{9,... | collective-permute-start | bytes 393224 | tf_op jit(solution)/shard_map/ppermute | solution.py:214
  66.3 17.8 %collective-permute-start.9 = (bf16[16,4096]{1,0:T(8,128)(2,1)S(1)}, bf16[16,4096]{1,0:T(8,128)(2,1)S(1)}, u32[]{:S(2)}, u32[]{:S(2)}) collective-permute-start(bf16[16,4096]{1,0:T(8,128)(2,1)S(1)} %add_convert_fusion), channel_id=1, source_target_pairs={{0,8},{4,12},{8,16},{12,20},{16,24},{20,28},{1,9},{5,13},{9,17},{1... | collective-permute-start | bytes 393224 | tf_op jit(solution)/shard_map/ppermute | solution.py:214
  70.2 2.2 %copy-start.4 = (f32[16,256]{1,0:T(8,128)S(1)}, f32[16,256]{1,0:T(8,128)}, u32[]{:S(2)}) copy-start(f32[16,256]{1,0:T(8,128)} %get-tuple-element.26) | copy-start | bytes 49156

commit v2 on v1

--- a/solution.py
+++ b/solution.py
@@ -159,7 +159,22 @@
         jnp.bfloat16
     )
     taps = jnp.repeat(short_taps, GROUP, axis=2)
-    rates_wide = jnp.repeat(decay_rates, GROUP, axis=1)
+    rates_wide = lax.optimization_barrier(jnp.repeat(decay_rates, GROUP, axis=1))
+    ends = jnp.cumsum(doc_lengths)
+    begins = ends - doc_lengths
+
+    def start_of(position):
+        return jnp.max(jnp.where(begins <= position, begins, 0))
+
+    last_own = start_of(begin + rows - 1)
+    last_before = start_of(jnp.maximum(begin - 1, 0))
+    span_begin = ctx_index * span
+    last_span = start_of(span_begin + span - 1)
+    edge_kv, edge_q, decay, own_rows, tail, taps, rates_wide, medium_rows, last_own, last_before, last_span = (
+        lax.optimization_barrier(
+            (edge_kv, edge_q, decay, own_rows, tail, taps, rates_wide, medium_rows, last_own, last_before, last_span)
+        )
+    )
 
     smem = pl.BlockSpec(memory_space=pltpu.SMEM)
     tile = lambda part=0: block((rows, TILE), lambda i: (0, i + part * tiles))
@@ -181,41 +196,6 @@
 
     before = lax.ppermute(product, everyone, pairs)
 
-    ends = jnp.cumsum(doc_lengths)
-    begins = ends - doc_lengths
-
-    def start_of(position):
-        return jnp.max(jnp.where(begins <= position, begins, 0))
-
-    def faded(distance, alive):
-        return jnp.where(alive, jnp.exp(-rates_wide * (distance * jnp.float32(rows))), 0.0)
-
-    last_own = start_of(begin + rows - 1)
-    last_before = start_of(jnp.maximum(begin - 1, 0))
-    span_begin = ctx_index * span
-    last_span = start_of(span_begin + span - 1)
-    to_end = (ts_count - 1 - ts_index).astype(jnp.float32)
-    step_in = faded(1.0, last_own < begin)
-    running, entered = state, jnp.zeros_like(state)
-    rest = state * faded(to_end, last_span <= begin + rows - 1)
-    for hop in range(ts_count - 1):
-        got = lax.ppermute(running.astype(jnp.bfloat16), "ts", [(hop, hop + 1)])
-        back_hop = ts_count - 1 - hop
-        got_rest = lax.ppermute(rest.astype(jnp.bfloat16), "ts", [(back_hop, back_hop - 1)])
-        got = got.astype(jnp.float32)
-        entered = entered + got
-        running = running + step_in * got
-        rest = rest + got_rest.astype(jnp.float32)
-    whole = rest + faded(to_end + 1.0, last_span < begin) * entered
-    whole = whole.astype(jnp.bfloat16)
-    for hop in range(1, reach + 1):
-        if hop >= ctx_count:
-            break
-        got = lax.ppermute(whole, "ctx", [(i, i + hop) for i in range(ctx_count - hop)])
-        distance = (ts_index + (hop - 1) * ts_count).astype(jnp.float32)
-        alive = last_before <= span_begin - (hop - 1) * span - 1
-        entered = entered + faded(distance, alive) * got.astype(jnp.float32)
-
     partial, query = pl.pallas_call(
         local_kernel,
         grid=(tiles,),
@@ -228,10 +208,39 @@
             pltpu.VMEM((2, rows, PER * LANES), jnp.bfloat16),
         ],
         cost_estimate=pl.CostEstimate(
-            flops=2 * rows * rows * width * PER, bytes_accessed=rows * width * 12, transcendentals=0
+            flops=16 * rows * rows * width * PER, bytes_accessed=rows * width * 12, transcendentals=0
         ),
         name="local",
     )(doc_lengths, begin_array, product, projected, edge_q, taps, own_rows, skip_gain[None])
+
+    def faded(distance, alive):
+        return jnp.where(alive, jnp.exp(-rates_wide * (distance * jnp.float32(rows))), 0.0)
+
+    to_end = (ts_count - 1 - ts_index).astype(jnp.float32)
+    step_in = faded(1.0, last_own < begin)
+    running, entered = state, jnp.zeros_like(state)
+    rest = state * faded(to_end, last_span <= begin + rows - 1)
+    for hop in range(ts_count - 1):
+        got = lax.ppermute(running.astype(jnp.bfloat16), "ts", [(hop, hop + 1)])
+        back_hop = ts_count - 1 - hop
+        got_rest = lax.ppermute(rest.astype(jnp.bfloat16), "ts", [(back_hop, back_hop - 1)])
+        got = got.astype(jnp.float32)
+        entered = entered + got
+        if hop == 0:
+            got, got_rest, partial, query = lax.optimization_barrier(
+                (got, got_rest, partial, query)
+            )
+        running = running + step_in * got
+        rest = rest + got_rest.astype(jnp.float32)
+    whole = rest + faded(to_end + 1.0, last_span < begin) * entered
+    whole = whole.astype(jnp.bfloat16)
+    for hop in range(1, reach + 1):
+        if hop >= ctx_count:
+            break
+        got = lax.ppermute(whole, "ctx", [(i, i + hop) for i in range(ctx_count - hop)])
+        distance = (ts_index + (hop - 1) * ts_count).astype(jnp.float32)
+        alive = last_before <= span_begin - (hop - 1) * span - 1
+        entered = entered + faded(distance, alive) * got.astype(jnp.float32)
 
     return pl.pallas_call(
         final_kernel,

time: 97.1 us -> 110 us (1.13)
  waiting for transfers between devices: 1.88 us -> 34.5 us
  local copies, waits for them, and re-layouts: 20.9 us -> 10.8 us
  starting transfers between devices: 30.2 us -> 24.1 us
  other arithmetic: 12 us -> 8.95 us
    ppermute x1, waiting for transfers between devices: 1.85 us -> 24.2 us  [per_device(): before = lax.ppermute(product, everyone, pairs)]
    ppermute x3, waiting for transfers between devices: 0.01 us -> 10.3 us  [per_device(): lax.ppermute(rest.astype(jnp.bfloat16), 'ts', [(back_hop, back_hop - 1)])]
    select_n x5 -> x0, local copies, waits for them, and re-layouts: 7.79 us -> none  [faded(): jnp.where(alive, jnp.exp(-rates_wide * (distance * jnp.float32(rows))), 0.0)]
    broadcast_in_dim x5 -> x1, local copies, waits for them, and re-layouts: 3.74 us -> 0.6 us  [per_device(): jnp.repeat(decay_rates, GROUP, axis=1)]
    ppermute x1, starting transfers between devices: 4.96 us -> 1.92 us  [per_device(): before = lax.ppermute(product, everyone, pairs)]
    ppermute x2, starting transfers between devices: 9.92 us -> 7.63 us  [per_device(): lax.ppermute(whole, 'ctx', [(i, i + hop) for i in range(ctx_count - hop)])]
    reshape x0 -> x1, local copies, waits for them, and re-layouts: none -> 1.56 us  [per_device(): jnp.repeat(decay_rates, GROUP, axis=1)]
    select_n x1 -> x0, other arithmetic: 1.38 us -> none  [faded(): jnp.where(alive, jnp.exp(-rates_wide * (distance * jnp.float32(rows))), 0.0)]
  transfers between devices with their start and end apart: 11 -> 11, of which waited for: 1 -> 2; matrix products, arithmetic and copies ran while one was open for 31% -> 15% of each run, Pallas kernels for 10% -> 9%
where the time goes in v2:
time: 110 us; the launch traced here: 109 us
  waiting for transfers between devices  34.5 us (31%)
  Pallas kernels  27.5 us (25%)
  starting transfers between devices  24.1 us (22%)
  local copies, waits for them, and re-layouts  10.8 us (10%)
  other arithmetic  8.95 us (8%)
  between operations  3.49 us (3%)
    ppermute x1, waiting for transfers between devices, per_device(): before = lax.ppermute(product, everyone, pairs)  24.2 us
    ppermute x3, waiting for transfers between devices, per_device(): lax.ppermute(rest.astype(jnp.bfloat16), 'ts', [(back_hop, back_hop - 1)])  10.3 us
    pallas_call x1, Pallas kernels, per_device(): pl.pallas_call(local_kernel, grid=(tiles,), in_specs=[smem, smem, tile(),...  9.6 us
    pallas_call x1, Pallas kernels, per_device(): pl.pallas_call(final_kernel, grid=(tiles,), in_specs=[smem, smem, tile(),...  9.08 us
    pallas_call x1, Pallas kernels, per_device(): pl.pallas_call(product_kernel, grid=(tiles,), in_specs=[smem, smem, tile(...  8.8 us
    ppermute x2, starting transfers between devices, per_device(): lax.ppermute(whole, 'ctx', [(i, i + hop) for i in range(ctx_count - hop)])  7.63 us
    ppermute x3, starting transfers between devices, per_device(): got = lax.ppermute(running.astype(jnp.bfloat16), 'ts', [(hop, hop + 1)])  4.68 us
    ppermute x1, starting transfers between devices, per_device(): edge_kv = lax.ppermute(projected[rows - EDGE:, width:], everyone, pairs)  4.03 us
  transfers between devices with their start and end apart: 11, of which 2 were waited for; matrix products, arithmetic and copies ran while one was open for 15% of the time, Pallas kernels for 9%

profile of v2, /device:TPU:1, one launch (start us, length us, event | category | flops | bytes accessed | tf_op | source)
XLA Modules:
  0.0 109.3 jit_solution(12396536142905205046)
XLA Ops:
  0.0 0.9 slice.12
  0.9 4.0 %collective-permute-start = (bf16[8,8192]{1,0:T(8,128)(2,1)S(1)}, bf16[8,8192]{1,0:T(8,128)(2,1)S(1)}, u32[]{:S(2)}, u32[]{:S(2)}) collective-permute-start(bf16[8,8192]{1,0:T(8,128)(2,1)S(1)} %slice.12), channel_id=1, source_target_pairs={{0,1},{1,2},{2,3},{3,4},{4,5},{5,6},{6,7},{7,8},{8,9},{9,10},{10,1... | collective-permute-start | bytes 393224 | tf_op jit(solution)/shard_map/ppermute | solution.py:141
  5.0 0.8 slice.13
  5.8 3.2 %collective-permute-start.1 = (bf16[8,4096]{1,0:T(8,128)(2,1)S(1)}, bf16[8,4096]{1,0:T(8,128)(2,1)S(1)}, u32[]{:S(2)}, u32[]{:S(2)}) collective-permute-start(bf16[8,4096]{1,0:T(8,128)(2,1)S(1)} %slice.13), channel_id=1, source_target_pairs={{0,1},{1,2},{2,3},{3,4},{4,5},{5,6},{6,7},{7,8},{8,9},{9,10},{10,1... | collective-permute-start | bytes 196616 | tf_op jit(solution)/shard_map/ppermute | solution.py:142
  9.0 0.9 slice.15
  10.0 0.7 slice.14
  10.7 0.8 fusion.13
  11.4 0.1 copy.16
  11.5 0.1 mul.140
  11.6 0.1 copy.17
  11.7 0.1 neg.35
  11.8 0.1 copy.21
  11.9 0.0 copy-start.5
  12.0 0.0 copy-start.4
  12.0 0.2 rev.3
  12.2 0.1 copy.19
  12.3 1.5 %exponential_convert_fusion.tail = bf16[4096,128]{1,0:T(8,128)(2,1)} fusion(f32[128]{0:T(128)S(1)} %iota_subtract_fusion, f32[4096]{0:T(1024)S(1)} %neg.35), kind=kLoop, calls=%fused_computation | loop fusion | flops 1048576 | bytes 1065472 | tf_op jit(solution)/shard_map/convert_element_type | solution.py:157
  13.8 1.3 %multiply_convert_fusion.decay = bf16[128,4096]{1,0:T(8,128)(2,1)} fusion(f32[128]{0:T(128)S(1)} %iota_add_fusion, f32[4096]{0:T(1024)S(1)} %neg.35, f32[4096]{0:T(1024)S(1)} %mul.140), kind=kLoop, calls=%fused_computation.2 | loop fusion | flops 1572864 | bytes 1081856 | tf_op jit(solution)/shard_map/convert_element_type | solution.py:158
  15.2 1.2 %multiply_reduce_fusion = f32[256,128]{1,0:T(8,128)S(1)} fusion(f32[128]{0:T(128)S(1)} %fusion.6, f32[16,256]{1,0:T(8,128)S(1)} %get-tuple-element.51, f32[16,256]{1,0:T(8,128)S(1)} %get-tuple-element.53), kind=kLoop, calls=%fused_computation.1 | loop fusion | flops 1540096 | bytes 164352 | tf_op jit(solution)/shard_map/reduce_sum | solution.py:151
  16.4 0.8 fusion.12
  17.2 0.0 copy-done.5
  17.2 0.1 copy.20
  17.4 0.1 reduce
  17.5 0.0 copy-done.4
  17.5 0.8 broadcast_in_dim.32
  18.3 0.0 copy-start.3
  18.3 2.5 %reshape.75.taps = f32[3,7,4096]{2,1,0:T(8,128)} reshape(f32[3,7,256,16]{3,2,1,0:T(8,128)S(1)} %broadcast_in_dim.32) | data formatting | bytes 688128 | tf_op jit(solution)/shard_map/reshape | solution.py:161
  20.8 0.0 copy-done.3
  20.8 0.6 broadcast_in_dim.33
  21.4 1.6 %reshape.76 = f32[16,4096]{1,0:T(8,128)S(1)} reshape(f32[16,256,16]{2,1,0:T(8,128)S(1)} %broadcast_in_dim.33) | data formatting | bytes 524288 | tf_op jit(solution)/shard_map/reshape | solution.py:162
  22.9 0.7 fusion.10
  23.6 0.0 collective-permute-done.1.qe_ref
  23.6 0.0 collective-permute-done.ke_ref.ve_ref
  24.3 0.0 copy-done.2
  24.3 8.8 %product.1 = (bf16[128,4096]{1,0:T(8,128)(2,1)}, f32[16,4096]{1,0:T(8,128)}) custom-call(s32[16]{0:T(128)} %lengths.5, s32[1]{0:T(128)} %bitcast.begin, bf16[128,12288]{1,0:T(8,128)(2,1)} %q_ref.1, bf16[128,12288]{1,0:T(8,128)(2,1)} %q_ref.1, bf16[8,8192]{1,0:T(8,128)(2,1)} %copy-done.2, bf16[8,8192]{1,0:T(8,128)(2,1)} %copy-done.2, ...), custom_call_target="tpu_custom_call" | custom-call | tf_op jit(solution)/shard_map/product/pallas_call | solution.py:186
  33.1 1.1 %fusion.11 = (bf16[16,4096]{1,0:T(8,128)(2,1)S(1)}, f32[16,4096]{1,0:T(8,128)S(1)}, bf16[16,4096]{1,0:T(8,128)(2,1)S(1)}) fusion(f32[16,4096]{1,0:T(8,128)} %get-tuple-element.30, f32[]{:T(128)S(6)} %mul.157, f32[16,4096]{1,0:T(8,128)S(1)} %reshape.76, pred[]{:T(512)S(6)} %le.33), kind=kLoop, calls=%fused_computation.34 | loop fusion | flops 393216 | bytes 1048581 | tf_op jit(solution)/shard_map/convert_element_type | solution.py:226
  34.2 3.2 %collective-permute-start.3 = (bf16[16,4096]{1,0:T(8,128)(2,1)S(1)}, bf16[16,4096]{1,0:T(8,128)(2,1)S(1)}, u32[]{:S(2)}, u32[]{:S(2)}) collective-permute-start(bf16[16,4096]{1,0:T(8,128)(2,1)S(1)} %get-tuple-element.50), channel_id=1, source_target_pairs={{0,1},{4,5},{8,9},{12,13},{16,17},{20,21},{24,25},{28,29}} | collective-permute-start | bytes 393224 | tf_op jit(solution)/shard_map/ppermute | solution.py:224
  37.4 0.7 collective-permute-start.4
  38.1 0.0 copy-done.7
  38.1 0.0 copy-start
  38.1 9.6 %local.1 = (f32[128,4096]{1,0:T(8,128)}, f32[128,4096]{1,0:T(8,128)}) custom-call(s32[16]{0:T(128)} %lengths.5, s32[1]{0:T(128)} %bitcast.begin, bf16[128,4096]{1,0:T(8,128)(2,1)} %get-tuple-element.27.x_ref, bf16[128,12288]{1,0:T(8,128)(2,1)} %q_ref.1, bf16[8,4096]{1,0:T(8,128)(2,1)} %copy-done.7, f32[3,7,4096]{2,1,0:T(8,128)} %reshape.75.taps, ...), custom_call_target="tpu_custom_call" | custom-call | flops 8589934592 | bytes 6291456 | tf_op jit(solution)/shard_map/local/pallas_call | solution.py:199
  48.4 0.0 collective-permute-done.3
  48.4 0.0 collective-permute-done.4
  48.4 0.1 fusion.5
  48.5 0.8 collective-permute-start.5
  49.3 0.7 collective-permute-start.7
  50.0 0.0 collective-permute-done.5
  50.0 0.1 fusion.2
  50.1 0.7 collective-permute-start.6
  50.8 0.0 collective-permute-done.7
  50.9 1.3 %collective-permute-start.8 = (bf16[16,4096]{1,0:T(8,128)(2,1)S(1)}, bf16[16,4096]{1,0:T(8,128)(2,1)S(1)}, u32[]{:S(2)}, u32[]{:S(2)}) collective-permute-start(bf16[16,4096]{1,0:T(8,128)(2,1)S(1)} %fusion.4), channel_id=1, source_target_pairs={{1,0},{5,4},{9,8},{13,12},{17,16},{21,20},{25,24},{29,28}} | collective-permute-start | bytes 393224 | tf_op jit(solution)/shard_map/ppermute | solution.py:226
  52.8 0.0 collective-permute-done.6
  52.8 10.3 %collective-permute-done.8 = bf16[16,4096]{1,0:T(8,128)(2,1)S(1)} collective-permute-done((bf16[16,4096]{1,0:T(8,128)(2,1)S(1)}, bf16[16,4096]{1,0:T(8,128)(2,1)S(1)}, u32[]{:S(2)}, u32[]{:S(2)}) %collective-permute-start.8) | collective-permute-done | bytes 131104 | tf_op jit(solution)/shard_map/ppermute | solution.py:226
  63.1 0.2 add_convert_fusion
  63.2 3.1 %collective-permute-start.10 = (bf16[16,4096]{1,0:T(8,128)(2,1)S(1)}, bf16[16,4096]{1,0:T(8,128)(2,1)S(1)}, u32[]{:S(2)}, u32[]{:S(2)}) collective-permute-start(bf16[16,4096]{1,0:T(8,128)(2,1)S(1)} %add_convert_fusion), channel_id=1, source_target_pairs={{0,8},{4,12},{8,16},{12,20},{16,24},{20,28},{1,9},{5,13},{9,17},{1... | collective-permute-start | bytes 393224 | tf_op jit(solution)/shard_map/ppermute | solution.py:240
  66.4 4.5 %collective-permute-start.9 = (bf16[16,4096]{1,0:T(8,128)(2,1)S(1)}, bf16[16,4096]{1,0:T(8,128)(2,1)S(1)}, u32[]{:S(2)}, u32[]{:S(2)}) collective-permute-start(bf16[16,4096]{1,0:T(8,128)(2,1)S(1)} %add_convert_fusion), channel_id=1, source_target_pairs={{0,4},{4,8},{8,12},{12,16},{16,20},{20,24},{24,28},{1,5},{5,9},{9,... | collective-permute-start | bytes 393224 | tf_op jit(solution)/shard_map/ppermute | solution.py:240
  70.9 0.0 copy-done.6
  70.9 1.9 %collective-permute-start.2 = (bf16[128,4096]{1,0:T(8,128)(2,1)S(1)}, bf16[128,4096]{1,0:T(8,128)(2,1)S(1)}, u32[]{:S(2)}, u32[]{:S(2)}) collective-permute-start(bf16[128,4096]{1,0:T(8,128)(2,1)S(1)} %copy-done.6), channel_id=1, source_target_pairs={{0,1},{1,2},{2,3},{3,4},{4,5},{5,6},{6,7},{7,8},{8,9},{9,10},{10,1... | collective-permute-start | bytes 3145736 | tf_op jit(solution)/shard_map/ppermute | solution.py:197
  74.1 0.0 collective-permute-done.10
  74.1 0.0 collective-permute-done.9
  74.1 0.9 multiply_add_fusion.state
  75.0 24.2 %collective-permute-done.2.x_ref = bf16[128,4096]{1,0:T(8,128)(2,1)S(1)} collective-permute-done((bf16[128,4096]{1,0:T(8,128)(2,1)S(1)}, bf16[128,4096]{1,0:T(8,128)(2,1)S(1)}, u32[]{:S(2)}, u32[]{:S(2)}) %collective-permute-start.2) | collective-permute-done | bytes 1048608 | tf_op jit(solution)/shard_map/ppermute | solution.py:197
  99.2 1.0 copy-done.1
  100.2 9.1 %final.1 = bf16[128,4096]{1,0:T(8,128)(2,1)} custom-call(s32[16]{0:T(128)} %lengths.5, s32[1]{0:T(128)} %bitcast.begin, bf16[128,4096]{1,0:T(8,128)(2,1)} %copy-done.1, f32[256,128]{1,0:T(8,128)} %get-tuple-element.28.wheel, bf16[128,4096]{1,0:T(8,128)(2,1)} %multiply_convert_fusion.decay, f32[16,4096]{1,0:T(8,128)} %multiply_add_fusion.state, ...), custom_call_target="tpu_custom_call" | custom-call | tf_op jit(solution)/shard_map/final/pallas_call | solution.py:245
  (12 shorter events, 0.2 us)
Async XLA Ops:
  0.9 22.7 %collective-permute-start = (bf16[8,8192]{1,0:T(8,128)(2,1)S(1)}, bf16[8,8192]{1,0:T(8,128)(2,1)S(1)}, u32[]{:S(2)}, u32[]{:S(2)}) collective-permute-start(bf16[8,8192]{1,0:T(8,128)(2,1)S(1)} %slice.12), channel_id=1, source_target_pairs={{0,1},{1,2},{2,3},{3,4},{4,5},{5,6},{6,7},{7,8},{8,9},{9,10},{10,1... | collective-permute-start | bytes 393224 | tf_op jit(solution)/shard_map/ppermute | solution.py:141
  5.8 17.8 %collective-permute-start.1 = (bf16[8,4096]{1,0:T(8,128)(2,1)S(1)}, bf16[8,4096]{1,0:T(8,128)(2,1)S(1)}, u32[]{:S(2)}, u32[]{:S(2)}) collective-permute-start(bf16[8,4096]{1,0:T(8,128)(2,1)S(1)} %slice.13), channel_id=1, source_target_pairs={{0,1},{1,2},{2,3},{3,4},{4,5},{5,6},{6,7},{7,8},{8,9},{9,10},{10,1... | collective-permute-start | bytes 196616 | tf_op jit(solution)/shard_map/ppermute | solution.py:142
  11.9 5.3 %copy-start.5 = (s32[16]{0:T(128)S(1)}, s32[16]{0:T(128)}, u32[]{:S(2)}) copy-start(s32[16]{0:T(128)} %lengths.5) | copy-start | bytes 196
  12.0 5.5 %copy-start.4 = (f32[3,7,256]{2,1,0:T(8,128)S(1)}, f32[3,7,256]{2,1,0:T(8,128)}, u32[]{:S(2)}) copy-start(f32[3,7,256]{2,1,0:T(8,128)} %param.9) | copy-start | bytes 64516
  18.3 2.5 %copy-start.3 = (f32[16,256]{1,0:T(8,128)S(1)}, f32[16,256]{1,0:T(8,128)}, u32[]{:S(2)}) copy-start(f32[16,256]{1,0:T(8,128)} %param.11) | copy-start | bytes 49156
  23.6 14.5 %copy-start.7 = (bf16[8,4096]{1,0:T(8,128)(2,1)}, bf16[8,4096]{1,0:T(8,128)(2,1)S(1)}, u32[]{:S(2)}) copy-start(bf16[8,4096]{1,0:T(8,128)(2,1)S(1)} %collective-permute-done.1.qe_ref) | copy-start | bytes 196612
  23.6 0.7 copy-start.2
  34.2 14.1 %collective-permute-start.3 = (bf16[16,4096]{1,0:T(8,128)(2,1)S(1)}, bf16[16,4096]{1,0:T(8,128)(2,1)S(1)}, u32[]{:S(2)}, u32[]{:S(2)}) collective-permute-start(bf16[16,4096]{1,0:T(8,128)(2,1)S(1)} %get-tuple-element.50), channel_id=1, source_target_pairs={{0,1},{4,5},{8,9},{12,13},{16,17},{20,21},{24,25},{28,29}} | collective-permute-start | bytes 393224 | tf_op jit(solution)/shard_map/ppermute | solution.py:224
  37.4 11.0 %collective-permute-start.4 = (bf16[16,4096]{1,0:T(8,128)(2,1)S(1)}, bf16[16,4096]{1,0:T(8,128)(2,1)S(1)}, u32[]{:S(2)}, u32[]{:S(2)}) collective-permute-start(bf16[16,4096]{1,0:T(8,128)(2,1)S(1)} %get-tuple-element.46), channel_id=1, source_target_pairs={{3,2},{7,6},{11,10},{15,14},{19,18},{23,22},{27,26},{31,30}} | collective-permute-start | bytes 393224 | tf_op jit(solution)/shard_map/ppermute | solution.py:226
  38.1 10.3 %copy-start = (f32[16,4096]{1,0:T(8,128)S(1)}, f32[16,4096]{1,0:T(8,128)}, u32[]{:S(2)}) copy-start(f32[16,4096]{1,0:T(8,128)} %get-tuple-element.30) | copy-start | bytes 786436
  48.4 22.5 %copy-start.6 = (bf16[128,4096]{1,0:T(8,128)(2,1)S(1)}, bf16[128,4096]{1,0:T(8,128)(2,1)}, u32[]{:S(2)}) copy-start(bf16[128,4096]{1,0:T(8,128)(2,1)} %get-tuple-element.27.x_ref) | copy-start | bytes 3145732
  48.5 1.5 %collective-permute-start.5 = (bf16[16,4096]{1,0:T(8,128)(2,1)S(1)}, bf16[16,4096]{1,0:T(8,128)(2,1)S(1)}, u32[]{:S(2)}, u32[]{:S(2)}) collective-permute-start(bf16[16,4096]{1,0:T(8,128)(2,1)S(1)} %fusion.5), channel_id=1, source_target_pairs={{1,2},{5,6},{9,10},{13,14},{17,18},{21,22},{25,26},{29,30}} | collective-permute-start | bytes 393224 | tf_op jit(solution)/shard_map/ppermute | solution.py:224
  49.3 1.5 %collective-permute-start.7 = (bf16[16,4096]{1,0:T(8,128)(2,1)S(1)}, bf16[16,4096]{1,0:T(8,128)(2,1)S(1)}, u32[]{:S(2)}, u32[]{:S(2)}) collective-permute-start(bf16[16,4096]{1,0:T(8,128)(2,1)S(1)} %fusion.3), channel_id=1, source_target_pairs={{2,1},{6,5},{10,9},{14,13},{18,17},{22,21},{26,25},{30,29}} | collective-permute-start | bytes 393224 | tf_op jit(solution)/shard_map/ppermute | solution.py:226
  50.1 2.7 %collective-permute-start.6 = (bf16[16,4096]{1,0:T(8,128)(2,1)S(1)}, bf16[16,4096]{1,0:T(8,128)(2,1)S(1)}, u32[]{:S(2)}, u32[]{:S(2)}) collective-permute-start(bf16[16,4096]{1,0:T(8,128)(2,1)S(1)} %fusion.2), channel_id=1, source_target_pairs={{2,3},{6,7},{10,11},{14,15},{18,19},{22,23},{26,27},{30,31}} | collective-permute-start | bytes 393224 | tf_op jit(solution)/shard_map/ppermute | solution.py:224
  50.9 12.2 %collective-permute-start.8 = (bf16[16,4096]{1,0:T(8,128)(2,1)S(1)}, bf16[16,4096]{1,0:T(8,128)(2,1)S(1)}, u32[]{:S(2)}, u32[]{:S(2)}) collective-permute-start(bf16[16,4096]{1,0:T(8,128)(2,1)S(1)} %fusion.4), channel_id=1, source_target_pairs={{1,0},{5,4},{9,8},{13,12},{17,16},{21,20},{25,24},{29,28}} | collective-permute-start | bytes 393224 | tf_op jit(solution)/shard_map/ppermute | solution.py:226
  63.2 10.9 %collective-permute-start.10 = (bf16[16,4096]{1,0:T(8,128)(2,1)S(1)}, bf16[16,4096]{1,0:T(8,128)(2,1)S(1)}, u32[]{:S(2)}, u32[]{:S(2)}) collective-permute-start(bf16[16,4096]{1,0:T(8,128)(2,1)S(1)} %add_convert_fusion), channel_id=1, source_target_pairs={{0,8},{4,12},{8,16},{12,20},{16,24},{20,28},{1,9},{5,13},{9,17},{1... | collective-permute-start | bytes 393224 | tf_op jit(solution)/shard_map/ppermute | solution.py:240
  66.4 7.7 %collective-permute-start.9 = (bf16[16,4096]{1,0:T(8,128)(2,1)S(1)}, bf16[16,4096]{1,0:T(8,128)(2,1)S(1)}, u32[]{:S(2)}, u32[]{:S(2)}) collective-permute-start(bf16[16,4096]{1,0:T(8,128)(2,1)S(1)} %add_convert_fusion), channel_id=1, source_target_pairs={{0,4},{4,8},{8,12},{12,16},{16,20},{20,24},{24,28},{1,5},{5,9},{9,... | collective-permute-start | bytes 393224 | tf_op jit(solution)/shard_map/ppermute | solution.py:240
  70.9 28.3 %collective-permute-start.2 = (bf16[128,4096]{1,0:T(8,128)(2,1)S(1)}, bf16[128,4096]{1,0:T(8,128)(2,1)S(1)}, u32[]{:S(2)}, u32[]{:S(2)}) collective-permute-start(bf16[128,4096]{1,0:T(8,128)(2,1)S(1)} %copy-done.6), channel_id=1, source_target_pairs={{0,1},{1,2},{2,3},{3,4},{4,5},{5,6},{6,7},{7,8},{8,9},{9,10},{10,1... | collective-permute-start | bytes 3145736 | tf_op jit(solution)/shard_map/ppermute | solution.py:197
  99.2 1.0 copy-start.1

commit v3 on v2

--- a/solution.py
+++ b/solution.py
@@ -121,6 +121,115 @@
         out[:, columns] = (query[:, columns] * filtered.astype(jnp.float32)).astype(jnp.bfloat16)
 
 
+def exchange_kernel(
+    ctx_count, ts_count, reach, rows, flags, product, state, rates, before, entered,
+    rest, run_out, run_in, rest_out, rest_in, whole_out, cross_in, send, recv
+):
+    ctx, ts = lax.axis_index("ctx"), lax.axis_index("ts")
+    me = ctx * ts_count + ts
+    has_before, has_after = me > 0, me < ctx_count * ts_count - 1
+    after, ahead = me + 1, me - 1 + ctx_count * ts_count
+
+    def place(index):
+        return (lax.rem(lax.div(index, ts_count), ctx_count), lax.rem(index, ts_count))
+
+    def copy(source, target, slot, device):
+        return pltpu.make_async_remote_copy(
+            src_ref=source, dst_ref=target, send_sem=send.at[slot], recv_sem=recv.at[slot],
+            device_id=device, device_id_type=pl.DeviceIdType.MESH,
+        )
+
+    def faded(distance, flag):
+        return jnp.exp(rates[...] * (-jnp.float32(rows) * distance)) * flags[flag]
+
+    barrier = pltpu.get_barrier_semaphore()
+
+    def greet(device):
+        pl.semaphore_signal(
+            barrier, inc=1, device_id=device, device_id_type=pl.DeviceIdType.MESH
+        )
+
+    above, below = lax.rem(ts + 1, ts_count), lax.rem(ts + ts_count - 1, ts_count)
+    hops = [k for k in range(1, reach + 1) if k < ctx_count]
+    pl.when(has_before)(lambda: greet(place(ahead)))
+    pl.when(ts < ts_count - 1)(lambda: greet((ctx, above)))
+    for k in hops:
+        pl.when(ctx >= k)(lambda k=k: greet((lax.rem(ctx + ctx_count - k, ctx_count), ts)))
+    peers = has_after.astype(jnp.int32) + (ts > 0).astype(jnp.int32)
+    for k in hops:
+        peers = peers + (ctx + k < ctx_count).astype(jnp.int32)
+    pl.semaphore_wait(barrier, peers)
+
+    main = copy(product, before, 0, place(after))
+    chain = copy(run_out, run_in, 1, (ctx, above))
+    suffix = copy(rest_out, rest_in, 2, (ctx, below))
+    cross = [
+        copy(whole_out, cross_in.at[k - 1], 2 + k, (lax.rem(ctx + k, ctx_count), ts))
+        for k in hops
+    ]
+    to_end = (ts_count - 1 - ts).astype(jnp.float32)
+    rest[...] = state[...] * faded(to_end, 1)
+    entered[...] = jnp.zeros_like(entered)
+
+    @pl.when(jnp.logical_not(has_before))
+    def _():
+        before[...] = jnp.zeros_like(before)
+
+    pl.when(has_after)(main.start)
+
+    def forward():
+        @pl.when(ts > 0)
+        def _():
+            chain.wait_recv()
+            entered[...] = run_in[...].astype(jnp.float32)
+
+        @pl.when(ts < ts_count - 1)
+        def _():
+            run_out[...] = (state[...] + faded(1.0, 0) * entered[...]).astype(jnp.bfloat16)
+            chain.start()
+
+    def backward():
+        @pl.when(ts < ts_count - 1)
+        def _():
+            suffix.wait_recv()
+            rest[...] = rest[...] + rest_in[...].astype(jnp.float32)
+
+        @pl.when(ts > 0)
+        def _():
+            rest_out[...] = rest[...].astype(jnp.bfloat16)
+            suffix.start()
+
+    late = ts >= ts_count // 2
+
+    @pl.when(late)
+    def _():
+        backward()
+        forward()
+
+    @pl.when(jnp.logical_not(late))
+    def _():
+        forward()
+        backward()
+
+    whole_out[...] = (rest[...] + faded(to_end + 1.0, 2) * entered[...]).astype(jnp.bfloat16)
+    for k, one in zip(hops, cross):
+        pl.when(ctx + k < ctx_count)(one.start)
+    for k, one in zip(hops, cross):
+        @pl.when(ctx >= k)
+        def _(k=k, one=one):
+            one.wait_recv()
+            distance = (ts + (k - 1) * ts_count).astype(jnp.float32)
+            entered[...] = entered[...] + faded(distance, 2 + k) * cross_in[k - 1].astype(
+                jnp.float32
+            )
+    pl.when(has_before)(main.wait_recv)
+    pl.when(has_after)(main.wait_send)
+    pl.when(ts < ts_count - 1)(chain.wait_send)
+    pl.when(ts > 0)(suffix.wait_send)
+    for k, one in zip(hops, cross):
+        pl.when(ctx + k < ctx_count)(one.wait_send)
+
+
 def block(shape, index):
     return pl.BlockSpec(shape, index)
 
@@ -194,7 +303,27 @@
         name="product",
     )(doc_lengths, begin_array, projected, projected, edge_kv, edge_kv, taps, tail)
 
-    before = lax.ppermute(product, everyone, pairs)
+    alive = [last_own < begin, last_span <= begin + rows - 1, last_span < begin] + [
+        last_before <= span_begin - hop * span - 1 for hop in range(reach)
+    ]
+    flags = jnp.stack(alive).astype(jnp.float32)
+    vmem = pl.BlockSpec(memory_space=pltpu.VMEM)
+    held = pltpu.VMEM((MODES, width), jnp.bfloat16)
+    before, entered = pl.pallas_call(
+        functools.partial(exchange_kernel, ctx_count, ts_count, reach, rows),
+        in_specs=[smem, vmem, vmem, vmem],
+        out_specs=[vmem, vmem],
+        out_shape=[wide(jnp.bfloat16), jax.ShapeDtypeStruct((MODES, width), jnp.float32)],
+        scratch_shapes=[
+            pltpu.VMEM((MODES, width), jnp.float32), held, held, held, held, held,
+            pltpu.VMEM((reach, MODES, width), jnp.bfloat16),
+            pltpu.SemaphoreType.DMA((3 + reach,)), pltpu.SemaphoreType.DMA((3 + reach,)),
+        ],
+        compiler_params=pltpu.CompilerParams(
+            collective_id=0, has_side_effects=True, vmem_limit_bytes=32 * 2**20
+        ),
+        name="exchange",
+    )(flags, product, state, rates_wide)
 
     partial, query = pl.pallas_call(
         local_kernel,
@@ -213,35 +342,6 @@
         name="local",
     )(doc_lengths, begin_array, product, projected, edge_q, taps, own_rows, skip_gain[None])
 
-    def faded(distance, alive):
-        return jnp.where(alive, jnp.exp(-rates_wide * (distance * jnp.float32(rows))), 0.0)
-
-    to_end = (ts_count - 1 - ts_index).astype(jnp.float32)
-    step_in = faded(1.0, last_own < begin)
-    running, entered = state, jnp.zeros_like(state)
-    rest = state * faded(to_end, last_span <= begin + rows - 1)
-    for hop in range(ts_count - 1):
-        got = lax.ppermute(running.astype(jnp.bfloat16), "ts", [(hop, hop + 1)])
-        back_hop = ts_count - 1 - hop
-        got_rest = lax.ppermute(rest.astype(jnp.bfloat16), "ts", [(back_hop, back_hop - 1)])
-        got = got.astype(jnp.float32)
-        entered = entered + got
-        if hop == 0:
-            got, got_rest, partial, query = lax.optimization_barrier(
-                (got, got_rest, partial, query)
-            )
-        running = running + step_in * got
-        rest = rest + got_rest.astype(jnp.float32)
-    whole = rest + faded(to_end + 1.0, last_span < begin) * entered
-    whole = whole.astype(jnp.bfloat16)
-    for hop in range(1, reach + 1):
-        if hop >= ctx_count:
-            break
-        got = lax.ppermute(whole, "ctx", [(i, i + hop) for i in range(ctx_count - hop)])
-        distance = (ts_index + (hop - 1) * ts_count).astype(jnp.float32)
-        alive = last_before <= span_begin - (hop - 1) * span - 1
-        entered = entered + faded(distance, alive) * got.astype(jnp.float32)
-
     return pl.pallas_call(
         final_kernel,
         grid=(tiles,),

time: 110 us -> 104 us (0.945)
  Pallas kernels: 27.5 us -> 72 us
  waiting for transfers between devices: 34.5 us -> 0.01 us
  starting transfers between devices: 24.1 us -> 7.22 us
  local copies, waits for them, and re-layouts: 10.8 us -> 12.9 us
  other arithmetic: 8.95 us -> 7.09 us
    pallas_call x0 -> x1, Pallas kernels: none -> 44.4 us  [per_device(): pl.pallas_call(functools.partial(exchange_kernel, ctx_count, ts_count, re...]
    ppermute x9 -> x0, waiting for transfers between devices: 34.5 us -> none  [the longest x1 24.2 us: per_device(): before = lax.ppermute(product, everyone, pairs)]
    ppermute x9 -> x0, starting transfers between devices: 16.9 us -> none  [the longest x2 7.63 us: per_device(): lax.ppermute(whole, 'ctx', [(i, i + hop) for i in range(ctx_count - hop)])]
    convert_element_type x7 -> x1, other arithmetic: 1.52 us -> 0.01 us  [per_device(): flags = jnp.stack(alive).astype(jnp.float32)]
  transfers between devices with their start and end apart: 11 -> 2, of which waited for: 2 -> 0; matrix products, arithmetic and copies ran while one was open for 15% -> 16% of each run, Pallas kernels for 9% -> 0%
where the time goes in v3:
time: 104 us; the launch traced here: 103 us
  Pallas kernels  72 us (69%)
  local copies, waits for them, and re-layouts  12.9 us (12%)
  starting transfers between devices  7.22 us (7%)
  other arithmetic  7.09 us (7%)
  between operations  3.34 us (3%)
    pallas_call x1, Pallas kernels, per_device(): pl.pallas_call(functools.partial(exchange_kernel, ctx_count, ts_count, re...  44.4 us
    pallas_call x1, Pallas kernels, per_device(): pl.pallas_call(local_kernel, grid=(tiles,), in_specs=[smem, smem, tile(),...  9.7 us
    pallas_call x1, Pallas kernels, per_device(): pl.pallas_call(final_kernel, grid=(tiles,), in_specs=[smem, smem, tile(),...  9.08 us
    pallas_call x1, Pallas kernels, per_device(): pl.pallas_call(product_kernel, grid=(tiles,), in_specs=[smem, smem, tile(...  8.81 us
    ppermute x1, starting transfers between devices, per_device(): edge_kv = lax.ppermute(projected[rows - EDGE:, width:], everyone, pairs)  4.02 us
    ppermute x1, starting transfers between devices, per_device(): edge_q = lax.ppermute(projected[rows - EDGE:, :width], everyone, pairs)  3.19 us
    reshape x1, local copies, waits for them, and re-layouts, per_device(): taps = jnp.repeat(short_taps, GROUP, axis=2)  2.52 us
  transfers between devices with their start and end apart: 2, of which 0 were waited for; matrix products, arithmetic and copies ran while one was open for 16% of the time, Pallas kernels for 0%

profile of v3, /device:TPU:1, one launch (start us, length us, event | category | flops | bytes accessed | tf_op | source)
XLA Modules:
  0.0 102.5 jit_solution(8687266752404605653)
XLA Ops:
  0.0 1.6 %slice.12 = bf16[8,8192]{1,0:T(8,128)(2,1)} slice(bf16[128,12288]{1,0:T(8,128)(2,1)} %q_ref.1), slice={[120:128], [4096:12288]} | slice | bytes 262144 | tf_op jit(solution)/shard_map/slice | solution.py:250
  1.6 4.0 %collective-permute-start = (bf16[8,8192]{1,0:T(8,128)(2,1)}, bf16[8,8192]{1,0:T(8,128)(2,1)S(1)}, u32[]{:S(2)}, u32[]{:S(2)}) collective-permute-start(bf16[8,8192]{1,0:T(8,128)(2,1)} %slice.12), channel_id=1, source_target_pairs={{0,1},{1,2},{2,3},{3,4},{4,5},{5,6},{6,7},{7,8},{8,9},{9,10},{10,1... | collective-permute-start | bytes 393224 | tf_op jit(solution)/shard_map/ppermute | solution.py:250
  5.6 1.5 %slice.13 = bf16[8,4096]{1,0:T(8,128)(2,1)} slice(bf16[128,12288]{1,0:T(8,128)(2,1)} %q_ref.1), slice={[120:128], [0:4096]} | slice | bytes 131072 | tf_op jit(solution)/shard_map/slice | solution.py:251
  7.1 3.2 %collective-permute-start.1 = (bf16[8,4096]{1,0:T(8,128)(2,1)}, bf16[8,4096]{1,0:T(8,128)(2,1)}, u32[]{:S(2)}, u32[]{:S(2)}) collective-permute-start(bf16[8,4096]{1,0:T(8,128)(2,1)} %slice.13), channel_id=1, source_target_pairs={{0,1},{1,2},{2,3},{3,4},{4,5},{5,6},{6,7},{7,8},{8,9},{9,10},{10,1... | collective-permute-start | bytes 196616 | tf_op jit(solution)/shard_map/ppermute | solution.py:251
  10.3 0.9 slice.15
  11.2 0.7 slice.14
  11.9 0.8 fusion.6
  12.7 0.1 copy.16
  12.8 0.1 mul.80
  12.9 0.1 copy.17
  13.0 0.1 neg.28
  13.1 0.1 copy.21
  13.2 0.0 copy-start.7
  13.2 0.0 copy-start.6
  13.2 0.2 rev.3
  13.4 0.1 copy.19
  13.6 1.5 %exponential_convert_fusion.tail = bf16[4096,128]{1,0:T(8,128)(2,1)} fusion(f32[128]{0:T(128)S(1)} %iota_subtract_fusion, f32[4096]{0:T(1024)S(1)} %neg.28), kind=kLoop, calls=%fused_computation | loop fusion | flops 1048576 | bytes 1065472 | tf_op jit(solution)/shard_map/convert_element_type | solution.py:266
  15.1 1.3 %multiply_convert_fusion.decay = bf16[128,4096]{1,0:T(8,128)(2,1)} fusion(f32[128]{0:T(128)S(1)} %iota_add_fusion, f32[4096]{0:T(1024)S(1)} %neg.28, f32[4096]{0:T(1024)S(1)} %mul.80), kind=kLoop, calls=%fused_computation.2 | loop fusion | flops 1572864 | bytes 1081856 | tf_op jit(solution)/shard_map/convert_element_type | solution.py:267
  16.4 1.2 %multiply_reduce_fusion = f32[256,128]{1,0:T(8,128)S(1)} fusion(f32[128]{0:T(128)S(1)} %fusion, f32[16,256]{1,0:T(8,128)S(1)} %get-tuple-element.44, f32[16,256]{1,0:T(8,128)S(1)} %get-tuple-element.46), kind=kLoop, calls=%fused_computation.1 | loop fusion | flops 1540096 | bytes 164352 | tf_op jit(solution)/shard_map/reduce_sum | solution.py:260
  17.7 0.8 fusion.5
  18.5 0.0 copy-done.7
  18.5 0.1 copy.20
  18.6 0.6 reduce
  19.3 0.0 copy-done.6
  19.3 0.8 broadcast_in_dim.24
  20.0 0.0 copy-start.5
  20.0 2.5 %reshape.75.taps = f32[3,7,4096]{2,1,0:T(8,128)} reshape(f32[3,7,256,16]{3,2,1,0:T(8,128)S(1)} %broadcast_in_dim.24) | data formatting | bytes 688128 | tf_op jit(solution)/shard_map/reshape | solution.py:270
  22.6 0.0 copy-done.5
  22.6 0.0 copy-start.8
  22.6 0.0 copy-start.9
  22.6 0.6 broadcast_in_dim.25
  23.2 1.6 %reshape.76.rates = f32[16,4096]{1,0:T(8,128)S(1)} reshape(f32[16,256,16]{2,1,0:T(8,128)S(1)} %broadcast_in_dim.25) | data formatting | bytes 524288 | tf_op jit(solution)/shard_map/reshape | solution.py:271
  24.7 0.0 copy-done.8
  24.7 0.0 copy-done.9
  24.7 0.7 fusion.4
  25.4 0.0 collective-permute-done.1.qe_ref
  25.4 0.0 collective-permute-done.ke_ref.ve_ref
  25.5 0.0 copy-start.4
  28.6 0.1 stack.23
  28.8 0.0 copy-done.4
  28.8 8.8 %product.1 = (bf16[128,4096]{1,0:T(8,128)(2,1)}, f32[16,4096]{1,0:T(8,128)}) custom-call(s32[16]{0:T(128)} %lengths.5, s32[1]{0:T(128)} %bitcast.begin, bf16[128,12288]{1,0:T(8,128)(2,1)} %q_ref.1, bf16[128,12288]{1,0:T(8,128)(2,1)} %q_ref.1, bf16[8,8192]{1,0:T(8,128)(2,1)} %copy-done.4, bf16[8,8192]{1,0:T(8,128)(2,1)} %copy-done.4, ...), custom_call_target="tpu_custom_call" | custom-call | tf_op jit(solution)/shard_map/product/pallas_call | solution.py:295
  37.6 0.0 copy-start
  37.6 0.0 copy-start.3
  37.6 9.7 %local.1 = (f32[128,4096]{1,0:T(8,128)}, f32[128,4096]{1,0:T(8,128)}) custom-call(s32[16]{0:T(128)} %lengths.5, s32[1]{0:T(128)} %bitcast.begin, bf16[128,4096]{1,0:T(8,128)(2,1)} %get-tuple-element.28.product.x_ref, bf16[128,12288]{1,0:T(8,128)(2,1)} %q_ref.1, bf16[8,4096]{1,0:T(8,128)(2,1)} %collective-permute-done.1.qe_ref, f32[3,7,4096]{2,1,0:T(8,128)} %reshape.75.taps, ...), custom_call_target="tpu_custom_call" | custom-call | flops 8589934592 | bytes 6291456 | tf_op jit(solution)/shard_map/local/pallas_call | solution.py:328
  47.3 0.0 copy-done
  47.3 0.0 copy-done.3
  47.3 44.4 %exchange.1 = (bf16[128,4096]{1,0:T(8,128)(2,1)S(1)}, f32[16,4096]{1,0:T(8,128)S(1)}) custom-call(f32[5]{0:T(128)S(1)} %convert_element_type.19.flags, bf16[128,4096]{1,0:T(8,128)(2,1)S(1)} %copy-done, f32[16,4096]{1,0:T(8,128)S(1)} %copy-done.3, f32[16,4096]{1,0:T(8,128)S(1)} %reshape.76.rates), custom_call_target="tpu_custom_call" | custom-call | tf_op jit(solution)/shard_map/exchange/pallas_call | solution.py:312
  91.7 0.0 copy-start.1
  91.7 1.0 copy-done.1
  92.7 0.0 copy-start.2
  92.7 0.7 copy-done.2
  93.4 9.1 %final.1 = bf16[128,4096]{1,0:T(8,128)(2,1)} custom-call(s32[16]{0:T(128)} %lengths.5, s32[1]{0:T(128)} %bitcast.begin, bf16[128,4096]{1,0:T(8,128)(2,1)} %copy-done.1, f32[256,128]{1,0:T(8,128)} %get-tuple-element.32.wheel, bf16[128,4096]{1,0:T(8,128)(2,1)} %multiply_convert_fusion.decay, f32[16,4096]{1,0:T(8,128)} %copy-done.2, ...), custom_call_target="tpu_custom_call" | custom-call | tf_op jit(solution)/shard_map/final/pallas_call | solution.py:345
  (5 shorter events, 0.1 us)
Async XLA Ops:
  1.6 23.9 %collective-permute-start = (bf16[8,8192]{1,0:T(8,128)(2,1)}, bf16[8,8192]{1,0:T(8,128)(2,1)S(1)}, u32[]{:S(2)}, u32[]{:S(2)}) collective-permute-start(bf16[8,8192]{1,0:T(8,128)(2,1)} %slice.12), channel_id=1, source_target_pairs={{0,1},{1,2},{2,3},{3,4},{4,5},{5,6},{6,7},{7,8},{8,9},{9,10},{10,1... | collective-permute-start | bytes 393224 | tf_op jit(solution)/shard_map/ppermute | solution.py:250
  7.1 18.4 %collective-permute-start.1 = (bf16[8,4096]{1,0:T(8,128)(2,1)}, bf16[8,4096]{1,0:T(8,128)(2,1)}, u32[]{:S(2)}, u32[]{:S(2)}) collective-permute-start(bf16[8,4096]{1,0:T(8,128)(2,1)} %slice.13), channel_id=1, source_target_pairs={{0,1},{1,2},{2,3},{3,4},{4,5},{5,6},{6,7},{7,8},{8,9},{9,10},{10,1... | collective-permute-start | bytes 196616 | tf_op jit(solution)/shard_map/ppermute | solution.py:251
  13.2 5.3 %copy-start.7 = (s32[16]{0:T(128)S(1)}, s32[16]{0:T(128)}, u32[]{:S(2)}) copy-start(s32[16]{0:T(128)} %lengths.5) | copy-start | bytes 196
  13.2 6.0 %copy-start.6 = (f32[3,7,256]{2,1,0:T(8,128)S(1)}, f32[3,7,256]{2,1,0:T(8,128)}, u32[]{:S(2)}) copy-start(f32[3,7,256]{2,1,0:T(8,128)} %param.9) | copy-start | bytes 64516
  20.0 2.5 %copy-start.5 = (f32[16,256]{1,0:T(8,128)S(1)}, f32[16,256]{1,0:T(8,128)}, u32[]{:S(2)}) copy-start(f32[16,256]{1,0:T(8,128)} %param.11) | copy-start | bytes 49156
  22.6 2.2 %copy-start.8 = (s32[16]{0:T(128)S(1)}, s32[16]{0:T(128)}, u32[]{:S(2)}) copy-start(s32[16]{0:T(128)} %lengths.5) | copy-start | bytes 196
  22.6 2.2 %copy-start.9 = (s32[16]{0:T(128)S(1)}, s32[16]{0:T(128)}, u32[]{:S(2)}) copy-start(s32[16]{0:T(128)} %reduce) | copy-start | bytes 196
  25.5 3.3 %copy-start.4 = (bf16[8,8192]{1,0:T(8,128)(2,1)}, bf16[8,8192]{1,0:T(8,128)(2,1)S(1)}, u32[]{:S(2)}) copy-start(bf16[8,8192]{1,0:T(8,128)(2,1)S(1)} %collective-permute-done.ke_ref.ve_ref) | copy-start | bytes 393220
  37.6 9.7 %copy-start = (bf16[128,4096]{1,0:T(8,128)(2,1)S(1)}, bf16[128,4096]{1,0:T(8,128)(2,1)}, u32[]{:S(2)}) copy-start(bf16[128,4096]{1,0:T(8,128)(2,1)} %get-tuple-element.28.product.x_ref) | copy-start | bytes 3145732
  37.6 9.7 %copy-start.3 = (f32[16,4096]{1,0:T(8,128)S(1)}, f32[16,4096]{1,0:T(8,128)}, u32[]{:S(2)}) copy-start(f32[16,4096]{1,0:T(8,128)} %get-tuple-element.29.state) | copy-start | bytes 786436
  91.7 1.0 copy-start.1
  92.7 0.7 copy-start.2

commit v4 on v3

--- a/solution.py
+++ b/solution.py
@@ -28,7 +28,7 @@
 
 def short_conv(value, edge, taps, part, valid, window, lane):
     rows = value.shape[0]
-    columns = pl.ds(lane * LANES, LANES)
+    columns = pl.ds(pl.multiple_of(lane * LANES, LANES), LANES)
     window[pl.ds(0, EDGE), :] = edge[:, columns].astype(jnp.float32)
     window[pl.ds(EDGE, rows), :] = value[:, columns].astype(jnp.float32)
     total = window[pl.ds(EDGE, rows), :] * taps[part, 0:1, columns]
@@ -80,22 +80,24 @@
         state[:, columns] = summed
 
 
-def local_kernel(
-    lengths, begin, x_ref, q_ref, qe_ref, taps, wheel, skip, partial, query, window, band
-):
-    rows = x_ref.shape[0]
-    start, position = row_starts(lengths, begin[0], rows)
+def local_part(lengths, begin, x_ref, q_ref, qe_ref, taps, wheel, skip, partial, query, window, band):
+    rows, width = x_ref.shape
+    start, position = row_starts(lengths, begin, rows)
     valid = position - start
     row = lax.broadcasted_iota(jnp.int32, (rows, LANES), 0)
     column = lax.broadcasted_iota(jnp.int32, (rows, LANES), 1)
-    mask = (column <= row) & (column + begin[0] >= start)
-    for lane in range(TILE // LANES):
-        columns = pl.ds(lane * LANES, LANES)
+    mask = (column <= row) & (column + begin >= start)
+
+    def one(lane, carry):
+        columns = pl.ds(pl.multiple_of(lane * LANES, LANES), LANES)
         query[:, columns] = short_conv(q_ref, qe_ref, taps, 0, valid, window, lane)
         block = x_ref[:, columns].astype(jnp.float32)
-        circulants(wheel, lane, mask, band.at[lane % 2])
-        summed = jnp.dot(band[lane % 2], spread(block), preferred_element_type=jnp.float32)
+        circulants(wheel, lane, mask, band)
+        summed = jnp.dot(band[...], spread(block), preferred_element_type=jnp.float32)
         partial[:, columns] = summed + skip[:, columns] * block
+        return carry
+
+    lax.fori_loop(0, width // LANES, one, 0)
 
 
 def final_kernel(
@@ -122,7 +124,8 @@
 
 
 def exchange_kernel(
-    ctx_count, ts_count, reach, rows, flags, product, state, rates, before, entered,
+    ctx_count, ts_count, reach, rows, lengths, flags, product, state, rates, q_ref, qe_ref, taps,
+    wheel, skip, before, entered, partial, query, window, band,
     rest, run_out, run_in, rest_out, rest_in, whole_out, cross_in, send, recv
 ):
     ctx, ts = lax.axis_index("ctx"), lax.axis_index("ts")
@@ -160,7 +163,10 @@
         peers = peers + (ctx + k < ctx_count).astype(jnp.int32)
     pl.semaphore_wait(barrier, peers)
 
-    main = copy(product, before, 0, place(after))
+    half = rows // 2
+    first, second = pl.ds(0, half), pl.ds(half, half)
+    main = copy(product.at[first], before.at[first], 0, place(after))
+    other = copy(product.at[second], before.at[second], 3 + reach, place(after))
     chain = copy(run_out, run_in, 1, (ctx, above))
     suffix = copy(rest_out, rest_in, 2, (ctx, below))
     cross = [
@@ -175,8 +181,6 @@
     def _():
         before[...] = jnp.zeros_like(before)
 
-    pl.when(has_after)(main.start)
-
     def forward():
         @pl.when(ts > 0)
         def _():
@@ -199,21 +203,29 @@
             rest_out[...] = rest[...].astype(jnp.bfloat16)
             suffix.start()
 
+    bottom, top = ts == 0, ts == ts_count - 1
     late = ts >= ts_count // 2
+    pl.when(bottom)(forward)
+    pl.when(top)(backward)
+    pl.when(has_after)(main.start)
+    local_part(
+        lengths, me * rows, product, q_ref, qe_ref, taps, wheel, skip, partial, query, window, band
+    )
 
     @pl.when(late)
     def _():
-        backward()
+        pl.when(jnp.logical_not(top))(backward)
         forward()
 
     @pl.when(jnp.logical_not(late))
     def _():
-        forward()
+        pl.when(jnp.logical_not(bottom))(forward)
         backward()
 
     whole_out[...] = (rest[...] + faded(to_end + 1.0, 2) * entered[...]).astype(jnp.bfloat16)
     for k, one in zip(hops, cross):
         pl.when(ctx + k < ctx_count)(one.start)
+    pl.when(has_after)(other.start)
     for k, one in zip(hops, cross):
         @pl.when(ctx >= k)
         def _(k=k, one=one):
@@ -222,8 +234,9 @@
             entered[...] = entered[...] + faded(distance, 2 + k) * cross_in[k - 1].astype(
                 jnp.float32
             )
-    pl.when(has_before)(main.wait_recv)
-    pl.when(has_after)(main.wait_send)
+    for one in (main, other):
+        pl.when(has_before)(one.wait_recv)
+        pl.when(has_after)(one.wait_send)
     pl.when(ts < ts_count - 1)(chain.wait_send)
     pl.when(ts > 0)(suffix.wait_send)
     for k, one in zip(hops, cross):
@@ -247,8 +260,7 @@
     tiles = width // TILE
     groups_tile = TILE // GROUP
 
-    edge_kv = lax.ppermute(projected[rows - EDGE :, width:], everyone, pairs)
-    edge_q = lax.ppermute(projected[rows - EDGE :, :width], everyone, pairs)
+    edges = lax.ppermute(projected[rows - EDGE :], everyone, pairs)
 
     begin = (ctx_index * ts_count + ts_index) * rows
     begin_array = jnp.full((1,), begin, jnp.int32)
@@ -279,9 +291,9 @@
     last_before = start_of(jnp.maximum(begin - 1, 0))
     span_begin = ctx_index * span
     last_span = start_of(span_begin + span - 1)
-    edge_kv, edge_q, decay, own_rows, tail, taps, rates_wide, medium_rows, last_own, last_before, last_span = (
+    edges, decay, own_rows, tail, taps, rates_wide, medium_rows, last_own, last_before, last_span = (
         lax.optimization_barrier(
-            (edge_kv, edge_q, decay, own_rows, tail, taps, rates_wide, medium_rows, last_own, last_before, last_span)
+            (edges, decay, own_rows, tail, taps, rates_wide, medium_rows, last_own, last_before, last_span)
         )
     )
 
@@ -295,13 +307,13 @@
     product, state = pl.pallas_call(
         product_kernel,
         grid=(tiles,),
-        in_specs=[smem, smem, tile(1), tile(2), edge(0), edge(1), taps_tile,
+        in_specs=[smem, smem, tile(1), tile(2), edge(1), edge(2), taps_tile,
                   block((TILE, rows), lambda i: (i, 0))],
         out_specs=[tile(), state_tile],
         out_shape=[wide(jnp.bfloat16), jax.ShapeDtypeStruct((MODES, width), jnp.float32)],
         scratch_shapes=[pltpu.VMEM((2, EDGE + rows, LANES), jnp.float32)],
         name="product",
-    )(doc_lengths, begin_array, projected, projected, edge_kv, edge_kv, taps, tail)
+    )(doc_lengths, begin_array, projected, projected, edges, edges, taps, tail)
 
     alive = [last_own < begin, last_span <= begin + rows - 1, last_span < begin] + [
         last_before <= span_begin - hop * span - 1 for hop in range(reach)
@@ -309,38 +321,26 @@
     flags = jnp.stack(alive).astype(jnp.float32)
     vmem = pl.BlockSpec(memory_space=pltpu.VMEM)
     held = pltpu.VMEM((MODES, width), jnp.bfloat16)
-    before, entered = pl.pallas_call(
+    before, entered, partial, query = pl.pallas_call(
         functools.partial(exchange_kernel, ctx_count, ts_count, reach, rows),
-        in_specs=[smem, vmem, vmem, vmem],
-        out_specs=[vmem, vmem],
-        out_shape=[wide(jnp.bfloat16), jax.ShapeDtypeStruct((MODES, width), jnp.float32)],
+        grid=(1,),
+        in_specs=[smem, smem, vmem, vmem, vmem, block((rows, width), lambda i: (0, 0)),
+                  block((EDGE, width), lambda i: (0, 0)), vmem, vmem, vmem],
+        out_specs=[vmem, vmem, vmem, vmem],
+        out_shape=[wide(jnp.bfloat16), jax.ShapeDtypeStruct((MODES, width), jnp.float32),
+                   wide(jnp.float32), wide(jnp.float32)],
         scratch_shapes=[
+            pltpu.VMEM((EDGE + rows, LANES), jnp.float32),
+            pltpu.VMEM((rows, PER * LANES), jnp.bfloat16),
             pltpu.VMEM((MODES, width), jnp.float32), held, held, held, held, held,
             pltpu.VMEM((reach, MODES, width), jnp.bfloat16),
-            pltpu.SemaphoreType.DMA((3 + reach,)), pltpu.SemaphoreType.DMA((3 + reach,)),
+            pltpu.SemaphoreType.DMA((4 + reach,)), pltpu.SemaphoreType.DMA((4 + reach,)),
         ],
         compiler_params=pltpu.CompilerParams(
             collective_id=0, has_side_effects=True, vmem_limit_bytes=32 * 2**20
         ),
         name="exchange",
-    )(flags, product, state, rates_wide)
-
-    partial, query = pl.pallas_call(
-        local_kernel,
-        grid=(tiles,),
-        in_specs=[smem, smem, tile(), tile(), edge(), taps_tile, wheel_tile,
-                  block((1, TILE), lambda i: (0, i))],
-        out_specs=[tile(), tile()],
-        out_shape=[wide(jnp.float32), wide(jnp.float32)],
-        scratch_shapes=[
-            pltpu.VMEM((EDGE + rows, LANES), jnp.float32),
-            pltpu.VMEM((2, rows, PER * LANES), jnp.bfloat16),
-        ],
-        cost_estimate=pl.CostEstimate(
-            flops=16 * rows * rows * width * PER, bytes_accessed=rows * width * 12, transcendentals=0
-        ),
-        name="local",
-    )(doc_lengths, begin_array, product, projected, edge_q, taps, own_rows, skip_gain[None])
+    )(doc_lengths, flags, product, state, rates_wide, projected, edges, taps, own_rows, skip_gain[None])
 
     return pl.pallas_call(
         final_kernel,

time: 104 us -> 106 us (1.019)
  local copies, waits for them, and re-layouts: 12.9 us -> 21.6 us
  Pallas kernels: 72 us -> 68 us
  starting transfers between devices: 7.22 us -> 4.03 us
    pallas_call x1 -> x0, Pallas kernels: 9.7 us -> none  [per_device(): pl.pallas_call(local_kernel, grid=(tiles,), in_specs=[smem, smem, tile(),...]
    unnamed x21 -> x35, local copies, waits for them, and re-layouts: 1.86 us -> 10.7 us
    pallas_call x1, Pallas kernels: 44.4 us -> 50 us  [per_device(): pl.pallas_call(functools.partial(exchange_kernel, ctx_count, ts_count, re...]
    ppermute x2 -> x1, starting transfers between devices: 7.22 us -> 4.03 us  [per_device(): edges = lax.ppermute(projected[rows - EDGE:], everyone, pairs)]
    slice x2 -> x1, local copies, waits for them, and re-layouts: 3.04 us -> 0.94 us  [per_device(): edges = lax.ppermute(projected[rows - EDGE:], everyone, pairs)]
  transfers between devices with their start and end apart: 2 -> 1, of which waited for: 0 -> 0; matrix products, arithmetic and copies ran while one was open for 16% -> 16% of each run, Pallas kernels for 0% -> 0%
where the time goes in v4:
time: 106 us; the launch traced here: 104 us
  Pallas kernels  68 us (64%)
  local copies, waits for them, and re-layouts  21.6 us (20%)
  other arithmetic  7.11 us (7%)
  starting transfers between devices  4.03 us (4%)
  between operations  3.16 us (3%)
    pallas_call x1, Pallas kernels, per_device(): pl.pallas_call(functools.partial(exchange_kernel, ctx_count, ts_count, re...  50 us
    unnamed x35, local copies, waits for them, and re-layouts  10.7 us
    pallas_call x1, Pallas kernels, per_device(): pl.pallas_call(final_kernel, grid=(tiles,), in_specs=[smem, smem, tile(),...  9.08 us
    pallas_call x1, Pallas kernels, per_device(): pl.pallas_call(product_kernel, grid=(tiles,), in_specs=[smem, smem, tile(...  8.97 us
    ppermute x1, starting transfers between devices, per_device(): edges = lax.ppermute(projected[rows - EDGE:], everyone, pairs)  4.03 us
    reshape x1, local copies, waits for them, and re-layouts, per_device(): taps = jnp.repeat(short_taps, GROUP, axis=2)  2.52 us
    reshape x1, local copies, waits for them, and re-layouts, per_device(): jnp.repeat(decay_rates, GROUP, axis=1)  2.25 us
  transfers between devices with their start and end apart: 1, of which 0 were waited for; matrix products, arithmetic and copies ran while one was open for 16% of the time, Pallas kernels for 0%

profile of v4, /device:TPU:1, one launch (start us, length us, event | category | flops | bytes accessed | tf_op | source)
XLA Modules:
  0.0 104.0 jit_solution(4704016919757000201)
XLA Ops:
  0.0 0.9 slice.9
  0.9 4.0 %collective-permute-start = (bf16[8,12288]{1,0:T(8,128)(2,1)S(1)}, bf16[8,12288]{1,0:T(8,128)(2,1)S(1)}, u32[]{:S(2)}, u32[]{:S(2)}) collective-permute-start(bf16[8,12288]{1,0:T(8,128)(2,1)S(1)} %slice.9), channel_id=1, source_target_pairs={{0,1},{1,2},{2,3},{3,4},{4,5},{5,6},{6,7},{7,8},{8,9},{9,10},{10,1... | collective-permute-start | bytes 589832 | tf_op jit(solution)/shard_map/ppermute | solution.py:263
  5.0 0.7 slice.10
  5.7 0.9 slice.11
  6.7 0.7 copy.20
  7.4 0.1 reduce
  7.5 0.1 copy.19
  7.7 0.8 fusion.6
  8.5 0.1 copy.17
  8.6 0.1 neg.28
  8.7 0.1 copy.16
  8.8 0.1 mul.80
  8.9 0.1 copy.21
  9.0 0.2 rev.3
  9.2 0.0 copy-start.16
  9.2 1.3 %broadcast_in_dim.25 = f32[16,256,16]{2,1,0:T(8,128)S(1)} broadcast(f32[16,256]{1,0:T(8,128)} %param.11), dimensions={0,1} | broadcast | bytes 278528 | tf_op jit(solution)/shard_map/broadcast_in_dim | solution.py:283
  10.5 2.3 %reshape.76.rates = f32[16,4096]{1,0:T(8,128)} reshape(f32[16,256,16]{2,1,0:T(8,128)S(1)} %broadcast_in_dim.25) | data formatting | bytes 524288 | tf_op jit(solution)/shard_map/reshape | solution.py:283
  12.8 0.0 copy-done.16
  12.8 0.8 broadcast_in_dim.24
  13.5 2.5 %reshape.75.taps = f32[3,7,4096]{2,1,0:T(8,128)} reshape(f32[3,7,256,16]{3,2,1,0:T(8,128)S(1)} %broadcast_in_dim.24) | data formatting | bytes 688128 | tf_op jit(solution)/shard_map/reshape | solution.py:282
  16.1 0.0 copy-start.13
  16.1 1.2 %multiply_reduce_fusion = f32[256,128]{1,0:T(8,128)S(1)} fusion(f32[128]{0:T(128)S(1)} %fusion, f32[16,256]{1,0:T(8,128)S(1)} %get-tuple-element.42, f32[16,256]{1,0:T(8,128)S(1)} %get-tuple-element.44), kind=kLoop, calls=%fused_computation.1 | loop fusion | flops 1540096 | bytes 164352 | tf_op jit(solution)/shard_map/reduce_sum | solution.py:272
  17.3 1.5 %exponential_convert_fusion.tail = bf16[4096,128]{1,0:T(8,128)(2,1)} fusion(f32[128]{0:T(128)S(1)} %iota_subtract_fusion, f32[4096]{0:T(1024)S(1)} %neg.28), kind=kLoop, calls=%fused_computation | loop fusion | flops 1048576 | bytes 1065472 | tf_op jit(solution)/shard_map/convert_element_type | solution.py:278
  18.8 1.4 %multiply_convert_fusion.decay = bf16[128,4096]{1,0:T(8,128)(2,1)} fusion(f32[128]{0:T(128)S(1)} %iota_add_fusion, f32[4096]{0:T(1024)S(1)} %neg.28, f32[4096]{0:T(1024)S(1)} %mul.80), kind=kLoop, calls=%fused_computation.2 | loop fusion | flops 1572864 | bytes 1081856 | tf_op jit(solution)/shard_map/convert_element_type | solution.py:279
  20.2 0.0 copy-done.13
  20.2 0.7 fusion.4
  20.9 0.8 fusion.5
  21.7 0.0 collective-permute-done.ke_ref.ve_ref.qe_ref
  21.7 0.0 copy-start.4
  24.7 0.1 stack.23
  24.8 0.5 convert_element_type.19.flags
  25.3 0.0 copy-done.4
  25.3 0.0 copy-start
  25.3 0.0 copy-start.1
  25.3 0.0 copy-start.12
  25.3 9.0 %product.1 = (bf16[128,4096]{1,0:T(8,128)(2,1)}, f32[16,4096]{1,0:T(8,128)}) custom-call(s32[16]{0:T(128)} %lengths.5, s32[1]{0:T(128)} %bitcast.begin, bf16[128,12288]{1,0:T(8,128)(2,1)} %q_ref.1, bf16[128,12288]{1,0:T(8,128)(2,1)} %q_ref.1, bf16[8,12288]{1,0:T(8,128)(2,1)} %copy-done.4, bf16[8,12288]{1,0:T(8,128)(2,1)} %copy-done.4, ...), custom_call_target="tpu_custom_call" | custom-call | tf_op jit(solution)/shard_map/product/pallas_call | solution.py:307
  34.3 0.0 copy-done
  34.3 0.0 copy-done.1
  34.3 0.0 copy-done.12
  34.3 0.0 copy-start.5
  34.4 0.9 copy-done.5
  35.3 0.0 copy-start.6
  35.3 0.9 copy-done.6
  36.2 0.0 copy-start.8
  36.2 1.2 %copy-done.8 = bf16[128,4096]{1,0:T(8,128)(2,1)S(1)} copy-done((bf16[128,4096]{1,0:T(8,128)(2,1)S(1)}, bf16[128,4096]{1,0:T(8,128)(2,1)}, u32[]{:S(2)}) %copy-start.8) | copy-done | bytes 1048600
  37.5 0.0 copy-start.9
  37.5 0.9 copy-done.9
  38.4 0.0 copy-start.11
  38.4 0.9 copy-done.11
  39.3 0.0 copy-start.14
  39.3 0.7 copy-done.14
  40.0 0.0 copy-start.15
  40.0 0.6 copy-done.15
  40.6 50.0 %exchange.1 = (bf16[128,4096]{1,0:T(8,128)(2,1)S(1)}, f32[16,4096]{1,0:T(8,128)S(1)}, f32[128,4096]{1,0:T(8,128)S(1)}, f32[128,4096]{1,0:T(8,128)S(1)}) custom-call(s32[16]{0:T(128)S(1)} %copy-done.14, f32[5]{0:T(128)S(1)} %copy-done.15, bf16[128,4096]{1,0:T(8,128)(2,1)S(1)} %copy-done.8, f32[16,4096]{1,0:T(8,128)S(1)} %copy-done.11, ...), custom_call_target="tpu_custom_call" | custom-call | tf_op jit(solution)/shard_map/exchange/pallas_call | solution.py:324
  90.6 0.0 copy-start.2
  90.6 1.3 %copy-done.2 = f32[128,4096]{1,0:T(8,128)} copy-done((f32[128,4096]{1,0:T(8,128)}, f32[128,4096]{1,0:T(8,128)S(1)}, u32[]{:S(2)}) %copy-start.2) | copy-done | bytes 2097176
  91.9 0.0 copy-start.3
  91.9 1.3 %copy-done.3 = f32[128,4096]{1,0:T(8,128)} copy-done((f32[128,4096]{1,0:T(8,128)}, f32[128,4096]{1,0:T(8,128)S(1)}, u32[]{:S(2)}) %copy-start.3) | copy-done | bytes 2097176
  93.2 0.0 copy-start.7
  93.2 1.0 copy-done.7
  94.2 0.0 copy-start.10
  94.2 0.7 copy-done.10
  94.9 9.1 %final.1 = bf16[128,4096]{1,0:T(8,128)(2,1)} custom-call(s32[16]{0:T(128)} %lengths.5, s32[1]{0:T(128)} %bitcast.begin, bf16[128,4096]{1,0:T(8,128)(2,1)} %copy-done.7, f32[256,128]{1,0:T(8,128)} %get-tuple-element.32.wheel, bf16[128,4096]{1,0:T(8,128)(2,1)} %multiply_convert_fusion.decay, f32[16,4096]{1,0:T(8,128)} %copy-done.10, f32[128,4096]{1,0:T(8,128)} %copy-done.2, ...), custom_call_target="tpu_custom_call" | custom-call | tf_op jit(solution)/shard_map/final/pallas_call | solution.py:345
  (4 shorter events, 0.1 us)
Async XLA Ops:
  0.9 20.8 %collective-permute-start = (bf16[8,12288]{1,0:T(8,128)(2,1)S(1)}, bf16[8,12288]{1,0:T(8,128)(2,1)S(1)}, u32[]{:S(2)}, u32[]{:S(2)}) collective-permute-start(bf16[8,12288]{1,0:T(8,128)(2,1)S(1)} %slice.9), channel_id=1, source_target_pairs={{0,1},{1,2},{2,3},{3,4},{4,5},{5,6},{6,7},{7,8},{8,9},{9,10},{10,1... | collective-permute-start | bytes 589832 | tf_op jit(solution)/shard_map/ppermute | solution.py:263
  9.2 3.6 %copy-start.16 = (f32[3,7,256]{2,1,0:T(8,128)S(1)}, f32[3,7,256]{2,1,0:T(8,128)}, u32[]{:S(2)}) copy-start(f32[3,7,256]{2,1,0:T(8,128)} %param.9) | copy-start | bytes 64516
  16.1 4.1 %copy-start.13 = (s32[16]{0:T(128)S(1)}, s32[16]{0:T(128)}, u32[]{:S(2)}) copy-start(s32[16]{0:T(128)} %lengths.5) | copy-start | bytes 196
  21.7 3.6 %copy-start.4 = (bf16[8,12288]{1,0:T(8,128)(2,1)}, bf16[8,12288]{1,0:T(8,128)(2,1)S(1)}, u32[]{:S(2)}) copy-start(bf16[8,12288]{1,0:T(8,128)(2,1)S(1)} %collective-permute-done.ke_ref.ve_ref.qe_ref) | copy-start | bytes 589828
  25.3 9.0 %copy-start = (bf16[128,12288]{1,0:T(8,128)(2,1)S(1)}, bf16[128,12288]{1,0:T(8,128)(2,1)}, u32[]{:S(2)}) copy-start(bf16[128,12288]{1,0:T(8,128)(2,1)} %q_ref.1) | copy-start | bytes 9437188
  25.3 9.0 %copy-start.1 = (f32[3,7,4096]{2,1,0:T(8,128)S(1)}, f32[3,7,4096]{2,1,0:T(8,128)}, u32[]{:S(2)}) copy-start(f32[3,7,4096]{2,1,0:T(8,128)} %reshape.75.taps) | copy-start | bytes 1032196
  25.3 9.0 %copy-start.12 = (f32[4096]{0:T(1024)S(1)}, f32[4096]{0:T(1024)}, u32[]{:S(2)}) copy-start(f32[4096]{0:T(1024)} %param.13) | copy-start | bytes 49156
  34.3 0.9 copy-start.5
  35.3 0.9 copy-start.6
  36.2 1.2 %copy-start.8 = (bf16[128,4096]{1,0:T(8,128)(2,1)S(1)}, bf16[128,4096]{1,0:T(8,128)(2,1)}, u32[]{:S(2)}) copy-start(bf16[128,4096]{1,0:T(8,128)(2,1)} %get-tuple-element.27.product) | copy-start | bytes 3145732
  37.5 0.9 copy-start.9
  38.4 0.9 copy-start.11
  39.3 0.7 copy-start.14
  40.0 0.6 copy-start.15
  90.6 1.3 %copy-start.2 = (f32[128,4096]{1,0:T(8,128)}, f32[128,4096]{1,0:T(8,128)S(1)}, u32[]{:S(2)}) copy-start(f32[128,4096]{1,0:T(8,128)S(1)} %get-tuple-element.35.partial) | copy-start | bytes 6291460
  91.9 1.3 %copy-start.3 = (f32[128,4096]{1,0:T(8,128)}, f32[128,4096]{1,0:T(8,128)S(1)}, u32[]{:S(2)}) copy-start(f32[128,4096]{1,0:T(8,128)S(1)} %get-tuple-element.36.query) | copy-start | bytes 6291460
  93.2 1.0 copy-start.7
  94.2 0.7 copy-start.10

commit v5 on v1

--- a/solution.py
+++ b/solution.py
@@ -138,8 +138,7 @@
     tiles = width // TILE
     groups_tile = TILE // GROUP
 
-    edge_kv = lax.ppermute(projected[rows - EDGE :, width:], everyone, pairs)
-    edge_q = lax.ppermute(projected[rows - EDGE :, :width], everyone, pairs)
+    edges = lax.ppermute(projected[rows - EDGE :], everyone, pairs)
 
     begin = (ctx_index * ts_count + ts_index) * rows
     begin_array = jnp.full((1,), begin, jnp.int32)
@@ -159,7 +158,7 @@
         jnp.bfloat16
     )
     taps = jnp.repeat(short_taps, GROUP, axis=2)
-    rates_wide = jnp.repeat(decay_rates, GROUP, axis=1)
+    rates_wide = lax.optimization_barrier(jnp.repeat(decay_rates, GROUP, axis=1))
 
     smem = pl.BlockSpec(memory_space=pltpu.SMEM)
     tile = lambda part=0: block((rows, TILE), lambda i: (0, i + part * tiles))
@@ -171,13 +170,13 @@
     product, state = pl.pallas_call(
         product_kernel,
         grid=(tiles,),
-        in_specs=[smem, smem, tile(1), tile(2), edge(0), edge(1), taps_tile,
+        in_specs=[smem, smem, tile(1), tile(2), edge(1), edge(2), taps_tile,
                   block((TILE, rows), lambda i: (i, 0))],
         out_specs=[tile(), state_tile],
         out_shape=[wide(jnp.bfloat16), jax.ShapeDtypeStruct((MODES, width), jnp.float32)],
         scratch_shapes=[pltpu.VMEM((2, EDGE + rows, LANES), jnp.float32)],
         name="product",
-    )(doc_lengths, begin_array, projected, projected, edge_kv, edge_kv, taps, tail)
+    )(doc_lengths, begin_array, projected, projected, edges, edges, taps, tail)
 
     before = lax.ppermute(product, everyone, pairs)
 
@@ -231,7 +230,7 @@
             flops=2 * rows * rows * width * PER, bytes_accessed=rows * width * 12, transcendentals=0
         ),
         name="local",
-    )(doc_lengths, begin_array, product, projected, edge_q, taps, own_rows, skip_gain[None])
+    )(doc_lengths, begin_array, product, projected, edges, taps, own_rows, skip_gain[None])
 
     return pl.pallas_call(
         final_kernel,

time: 97.1 us -> 103 us (1.061)
  starting transfers between devices: 30.2 us -> 52 us
  local copies, waits for them, and re-layouts: 20.9 us -> 8.72 us
  other arithmetic: 12 us -> 8.95 us
    ppermute x2, starting transfers between devices: 9.92 us -> 30.9 us  [per_device(): lax.ppermute(whole, 'ctx', [(i, i + hop) for i in range(ctx_count - hop)])]
    select_n x5 -> x0, local copies, waits for them, and re-layouts: 7.79 us -> none  [faded(): jnp.where(alive, jnp.exp(-rates_wide * (distance * jnp.float32(rows))), 0.0)]
    ppermute x1, starting transfers between devices: 4.96 us -> 10.8 us  [per_device(): before = lax.ppermute(product, everyone, pairs)]
    ppermute x2 -> x1, starting transfers between devices: 8.18 us -> 4.03 us  [per_device(): edges = lax.ppermute(projected[rows - EDGE:], everyone, pairs)]
    broadcast_in_dim x5 -> x1, local copies, waits for them, and re-layouts: 3.74 us -> 0.6 us  [per_device(): jnp.repeat(decay_rates, GROUP, axis=1)]
    ppermute x1, waiting for transfers between devices: 1.85 us -> 0.01 us  [per_device(): before = lax.ppermute(product, everyone, pairs)]
    reshape x0 -> x1, local copies, waits for them, and re-layouts: none -> 1.56 us  [per_device(): jnp.repeat(decay_rates, GROUP, axis=1)]
    slice x2 -> x1, local copies, waits for them, and re-layouts: 2.38 us -> 0.94 us  [per_device(): edges = lax.ppermute(projected[rows - EDGE:], everyone, pairs)]
  transfers between devices with their start and end apart: 11 -> 10, of which waited for: 1 -> 1; matrix products, arithmetic and copies ran while one was open for 31% -> 15% of each run, Pallas kernels for 10% -> 9%
where the time goes in v5:
time: 103 us; the launch traced here: 102 us
  starting transfers between devices  52 us (50%)
  Pallas kernels  27.5 us (27%)
  other arithmetic  8.95 us (9%)
  local copies, waits for them, and re-layouts  8.72 us (8%)
  between operations  3.64 us (4%)
  waiting for transfers between devices  1.04 us (1%)
    ppermute x2, starting transfers between devices, per_device(): lax.ppermute(whole, 'ctx', [(i, i + hop) for i in range(ctx_count - hop)])  30.9 us
    ppermute x1, starting transfers between devices, per_device(): before = lax.ppermute(product, everyone, pairs)  10.8 us
    pallas_call x1, Pallas kernels, per_device(): pl.pallas_call(local_kernel, grid=(tiles,), in_specs=[smem, smem, tile(),...  9.6 us
    pallas_call x1, Pallas kernels, per_device(): pl.pallas_call(final_kernel, grid=(tiles,), in_specs=[smem, smem, tile(),...  9.09 us
    pallas_call x1, Pallas kernels, per_device(): pl.pallas_call(product_kernel, grid=(tiles,), in_specs=[smem, smem, tile(...  8.82 us
    ppermute x1, starting transfers between devices, per_device(): edges = lax.ppermute(projected[rows - EDGE:], everyone, pairs)  4.03 us
    ppermute x3, starting transfers between devices, per_device(): got = lax.ppermute(running.astype(jnp.bfloat16), 'ts', [(hop, hop + 1)])  3.54 us
    ppermute x3, starting transfers between devices, per_device(): lax.ppermute(rest.astype(jnp.bfloat16), 'ts', [(back_hop, back_hop - 1)])  2.76 us
  transfers between devices with their start and end apart: 10, of which 1 were waited for; matrix products, arithmetic and copies ran while one was open for 15% of the time, Pallas kernels for 9%

profile of v5, /device:TPU:1, one launch (start us, length us, event | category | flops | bytes accessed | tf_op | source)
XLA Modules:
  0.0 101.8 jit_solution(5451774738750606595)
XLA Ops:
  0.0 0.9 slice.9
  0.9 4.0 %collective-permute-start = (bf16[8,12288]{1,0:T(8,128)(2,1)S(1)}, bf16[8,12288]{1,0:T(8,128)(2,1)S(1)}, u32[]{:S(2)}, u32[]{:S(2)}) collective-permute-start(bf16[8,12288]{1,0:T(8,128)(2,1)S(1)} %slice.9), channel_id=1, source_target_pairs={{0,1},{1,2},{2,3},{3,4},{4,5},{5,6},{6,7},{7,8},{8,9},{9,10},{10,1... | collective-permute-start | bytes 589832 | tf_op jit(solution)/shard_map/ppermute | solution.py:141
  5.0 0.8 sqrt_multiply_fusion
  5.8 0.1 copy.16
  5.9 0.1 neg.34
  6.0 1.5 %exponential_convert_fusion.tail = bf16[4096,128]{1,0:T(8,128)(2,1)} fusion(f32[128]{0:T(128)S(1)} %iota_subtract_fusion, f32[4096]{0:T(1024)S(1)} %neg.34), kind=kLoop, calls=%fused_computation.2 | loop fusion | flops 1048576 | bytes 1065472 | tf_op jit(solution)/shard_map/convert_element_type | solution.py:156
  7.5 1.5 %broadcast_in_dim.32 = f32[3,7,256,16]{3,2,1,0:T(8,128)S(1)} broadcast(f32[3,7,256]{2,1,0:T(8,128)} %param.9), dimensions={0,1,2} | broadcast | bytes 365568 | tf_op jit(solution)/shard_map/broadcast_in_dim | solution.py:160
  9.0 2.5 %reshape.75.taps = f32[3,7,4096]{2,1,0:T(8,128)} reshape(f32[3,7,256,16]{3,2,1,0:T(8,128)S(1)} %broadcast_in_dim.32) | data formatting | bytes 688128 | tf_op jit(solution)/shard_map/reshape | solution.py:160
  11.5 1.0 collective-permute-done.ke_ref.ve_ref.qe_ref
  12.5 0.0 copy-start.1
  12.5 0.7 copy-done.1
  13.2 0.0 copy-start.5
  13.2 0.0 copy-start.4
  13.2 8.8 %product.1 = (bf16[128,4096]{1,0:T(8,128)(2,1)}, f32[16,4096]{1,0:T(8,128)}) custom-call(s32[16]{0:T(128)} %lengths.5, s32[1]{0:T(128)} %bitcast.begin, bf16[128,12288]{1,0:T(8,128)(2,1)} %q_ref.1, bf16[128,12288]{1,0:T(8,128)(2,1)} %q_ref.1, bf16[8,12288]{1,0:T(8,128)(2,1)} %copy-done.1, bf16[8,12288]{1,0:T(8,128)(2,1)} %copy-done.1, ...), custom_call_target="tpu_custom_call" | custom-call | tf_op jit(solution)/shard_map/product/pallas_call | solution.py:170
  22.0 1.0 convert_element_type.69
  23.0 2.2 %collective-permute-start.2 = (bf16[16,4096]{1,0:T(8,128)(2,1)S(1)}, bf16[16,4096]{1,0:T(8,128)(2,1)S(1)}, u32[]{:S(2)}, u32[]{:S(2)}) collective-permute-start(bf16[16,4096]{1,0:T(8,128)(2,1)S(1)} %convert_element_type.69), channel_id=1, source_target_pairs={{0,1},{4,5},{8,9},{12,13},{16,17},{20,21},{24,25},{28,29}} | collective-permute-start | bytes 393224 | tf_op jit(solution)/shard_map/ppermute | solution.py:201
  25.2 0.0 copy-done.5
  25.2 0.1 copy.20
  25.3 0.1 reduce
  25.4 0.7 fusion.10
  26.8 0.0 copy-done.4
  26.9 0.0 copy-start
  26.9 0.6 broadcast_in_dim.34
  27.5 1.6 %reshape.78 = f32[16,4096]{1,0:T(8,128)S(1)} reshape(f32[16,256,16]{2,1,0:T(8,128)S(1)} %broadcast_in_dim.34) | data formatting | bytes 524288 | tf_op jit(solution)/shard_map/reshape | solution.py:161
  29.0 0.0 copy-start.3
  29.0 0.0 collective-permute-done.2
  29.0 0.0 copy-done
  29.0 0.1 fusion.5
  29.1 0.0 slice-start
  29.1 0.7 collective-permute-start.3
  30.4 0.0 collective-permute-done.3
  30.4 0.2 fusion.13
  30.6 0.7 collective-permute-start.5
  31.3 0.1 copy.19
  31.4 0.1 mul.143
  31.5 0.0 copy-start.2
  31.5 0.0 collective-permute-done.5
  31.6 0.8 collective-permute-start.6
  32.4 1.4 %multiply_convert_fusion.decay = bf16[128,4096]{1,0:T(8,128)(2,1)} fusion(f32[128]{0:T(128)S(1)} %iota_add_fusion, f32[4096]{0:T(1024)S(1)} %neg.34, f32[4096]{0:T(1024)S(1)} %mul.143), kind=kLoop, calls=%fused_computation.1 | loop fusion | flops 1572864 | bytes 1081856 | tf_op jit(solution)/shard_map/convert_element_type | solution.py:157
  34.4 0.0 copy-done.3
  34.4 0.1 copy.21
  34.5 0.2 rev.3
  34.7 0.0 slice-done
  34.7 0.1 copy.18
  34.9 0.7 collective-permute-start.4
  35.5 0.0 collective-permute-done.6
  35.6 1.3 %collective-permute-start.7 = (bf16[16,4096]{1,0:T(8,128)(2,1)S(1)}, bf16[16,4096]{1,0:T(8,128)(2,1)S(1)}, u32[]{:S(2)}, u32[]{:S(2)}) collective-permute-start(bf16[16,4096]{1,0:T(8,128)(2,1)S(1)} %fusion.6), channel_id=1, source_target_pairs={{1,0},{5,4},{9,8},{13,12},{17,16},{21,20},{25,24},{29,28}} | collective-permute-start | bytes 393224 | tf_op jit(solution)/shard_map/ppermute | solution.py:203
  36.9 1.2 %multiply_reduce_fusion = f32[256,128]{1,0:T(8,128)S(1)} fusion(f32[128]{0:T(128)S(1)} %fusion.7, f32[16,256]{1,0:T(8,128)S(1)} %get-tuple-element.23, f32[16,256]{1,0:T(8,128)S(1)} %get-tuple-element.21), kind=kLoop, calls=%fused_computation | loop fusion | flops 1540096 | bytes 164352 | tf_op jit(solution)/shard_map/reduce_sum | solution.py:150
  38.2 0.0 copy-done.2
  38.2 10.8 %collective-permute-start.1 = (bf16[128,4096]{1,0:T(8,128)(2,1)S(1)}, bf16[128,4096]{1,0:T(8,128)(2,1)}, u32[]{:S(2)}, u32[]{:S(2)}) collective-permute-start(bf16[128,4096]{1,0:T(8,128)(2,1)S(1)} %copy-done.2), channel_id=1, source_target_pairs={{0,1},{1,2},{2,3},{3,4},{4,5},{5,6},{6,7},{7,8},{8,9},{9,10},{10,1... | collective-permute-start | bytes 3145736 | tf_op jit(solution)/shard_map/ppermute | solution.py:181
  49.0 0.0 collective-permute-done.4
  49.0 0.0 collective-permute-done.7
  49.0 0.2 add_convert_fusion
  49.2 27.7 %collective-permute-start.8 = (bf16[16,4096]{1,0:T(8,128)(2,1)S(1)}, bf16[16,4096]{1,0:T(8,128)(2,1)S(1)}, u32[]{:S(2)}, u32[]{:S(2)}) collective-permute-start(bf16[16,4096]{1,0:T(8,128)(2,1)S(1)} %add_convert_fusion), channel_id=1, source_target_pairs={{0,4},{4,8},{8,12},{12,16},{16,20},{20,24},{24,28},{1,5},{5,9},{9,... | collective-permute-start | bytes 393224 | tf_op jit(solution)/shard_map/ppermute | solution.py:213
  76.9 3.1 %collective-permute-start.9 = (bf16[16,4096]{1,0:T(8,128)(2,1)S(1)}, bf16[16,4096]{1,0:T(8,128)(2,1)S(1)}, u32[]{:S(2)}, u32[]{:S(2)}) collective-permute-start(bf16[16,4096]{1,0:T(8,128)(2,1)S(1)} %add_convert_fusion), channel_id=1, source_target_pairs={{0,8},{4,12},{8,16},{12,20},{16,24},{20,28},{1,9},{5,13},{9,17},{1... | collective-permute-start | bytes 393224 | tf_op jit(solution)/shard_map/ppermute | solution.py:213
  80.0 0.8 fusion.12
  82.2 9.6 %local.1 = (f32[128,4096]{1,0:T(8,128)}, f32[128,4096]{1,0:T(8,128)}) custom-call(s32[16]{0:T(128)} %lengths.5, s32[1]{0:T(128)} %bitcast.begin, bf16[128,4096]{1,0:T(8,128)(2,1)} %get-tuple-element.9.x_ref, bf16[128,12288]{1,0:T(8,128)(2,1)} %q_ref.1, bf16[8,12288]{1,0:T(8,128)(2,1)} %copy-done.1, f32[3,7,4096]{2,1,0:T(8,128)} %reshape.75.taps, ...), custom_call_target="tpu_custom_call" | custom-call | flops 1073741824 | bytes 6291456 | tf_op jit(solution)/shard_map/local/pallas_call | solution.py:218
  91.8 0.0 collective-permute-done.8
  91.8 0.0 collective-permute-done.9
  91.8 0.9 multiply_add_fusion.state
  92.7 0.0 collective-permute-done.1.x_ref
  92.7 9.1 %final.1 = bf16[128,4096]{1,0:T(8,128)(2,1)} custom-call(s32[16]{0:T(128)} %lengths.5, s32[1]{0:T(128)} %bitcast.begin, bf16[128,4096]{1,0:T(8,128)(2,1)} %collective-permute-done.1.x_ref, f32[256,128]{1,0:T(8,128)} %get-tuple-element.17.wheel, bf16[128,4096]{1,0:T(8,128)(2,1)} %multiply_convert_fusion.decay, f32[16,4096]{1,0:T(8,128)} %multiply_add_fusion.state, ...), custom_call_target="tpu_custom_call" | custom-call | tf_op jit(solution)/shard_map/final/pallas_call | solution.py:235
  (7 shorter events, 0.1 us)
Async XLA Ops:
  0.9 11.6 %collective-permute-start = (bf16[8,12288]{1,0:T(8,128)(2,1)S(1)}, bf16[8,12288]{1,0:T(8,128)(2,1)S(1)}, u32[]{:S(2)}, u32[]{:S(2)}) collective-permute-start(bf16[8,12288]{1,0:T(8,128)(2,1)S(1)} %slice.9), channel_id=1, source_target_pairs={{0,1},{1,2},{2,3},{3,4},{4,5},{5,6},{6,7},{7,8},{8,9},{9,10},{10,1... | collective-permute-start | bytes 589832 | tf_op jit(solution)/shard_map/ppermute | solution.py:141
  12.5 0.7 copy-start.1
  13.2 12.0 %copy-start.5 = (s32[16]{0:T(128)S(1)}, s32[16]{0:T(128)}, u32[]{:S(2)}) copy-start(s32[16]{0:T(128)} %lengths.5) | copy-start | bytes 196
  13.2 13.6 %copy-start.4 = (f32[16,256]{1,0:T(8,128)S(1)}, f32[16,256]{1,0:T(8,128)}, u32[]{:S(2)}) copy-start(f32[16,256]{1,0:T(8,128)} %param.11) | copy-start | bytes 49156
  23.0 6.0 %collective-permute-start.2 = (bf16[16,4096]{1,0:T(8,128)(2,1)S(1)}, bf16[16,4096]{1,0:T(8,128)(2,1)S(1)}, u32[]{:S(2)}, u32[]{:S(2)}) collective-permute-start(bf16[16,4096]{1,0:T(8,128)(2,1)S(1)} %convert_element_type.69), channel_id=1, source_target_pairs={{0,1},{4,5},{8,9},{12,13},{16,17},{20,21},{24,25},{28,29}} | collective-permute-start | bytes 393224 | tf_op jit(solution)/shard_map/ppermute | solution.py:201
  26.9 2.2 %copy-start = (f32[16,4096]{1,0:T(8,128)S(1)}, f32[16,4096]{1,0:T(8,128)}, u32[]{:S(2)}) copy-start(f32[16,4096]{1,0:T(8,128)} %get-tuple-element.10) | copy-start | bytes 786436
  29.0 5.4 %copy-start.3 = (f32[128,256]{1,0:T(8,128)S(1)}, f32[128,256]{1,0:T(8,128)}, u32[]{:S(2)}) copy-start(f32[128,256]{1,0:T(8,128)} %param.10) | copy-start | bytes 393220
  29.1 5.6 %slice-start = ((f32[128,256]{1,0:T(8,128)}), f32[1,256]{1,0:T(1,128)S(1)}, s32[]{:S(2)}) async-start(f32[128,256]{1,0:T(8,128)} %param.10), calls=%async_computation | async-start | bytes 2048 | tf_op jit(solution)/shard_map/slice | solution.py:149
  29.1 1.3 %collective-permute-start.3 = (bf16[16,4096]{1,0:T(8,128)(2,1)S(1)}, bf16[16,4096]{1,0:T(8,128)(2,1)S(1)}, u32[]{:S(2)}, u32[]{:S(2)}) collective-permute-start(bf16[16,4096]{1,0:T(8,128)(2,1)S(1)} %fusion.5), channel_id=1, source_target_pairs={{1,2},{5,6},{9,10},{13,14},{17,18},{21,22},{25,26},{29,30}} | collective-permute-start | bytes 393224 | tf_op jit(solution)/shard_map/ppermute | solution.py:201
  30.6 0.9 collective-permute-start.5
  31.5 6.7 %copy-start.2 = (bf16[128,4096]{1,0:T(8,128)(2,1)S(1)}, bf16[128,4096]{1,0:T(8,128)(2,1)}, u32[]{:S(2)}) copy-start(bf16[128,4096]{1,0:T(8,128)(2,1)} %get-tuple-element.9.x_ref) | copy-start | bytes 3145732
  31.6 4.0 %collective-permute-start.6 = (bf16[16,4096]{1,0:T(8,128)(2,1)S(1)}, bf16[16,4096]{1,0:T(8,128)(2,1)S(1)}, u32[]{:S(2)}, u32[]{:S(2)}) collective-permute-start(bf16[16,4096]{1,0:T(8,128)(2,1)S(1)} %fusion.4), channel_id=1, source_target_pairs={{2,1},{6,5},{10,9},{14,13},{18,17},{22,21},{26,25},{30,29}} | collective-permute-start | bytes 393224 | tf_op jit(solution)/shard_map/ppermute | solution.py:203
  34.9 14.1 %collective-permute-start.4 = (bf16[16,4096]{1,0:T(8,128)(2,1)S(1)}, bf16[16,4096]{1,0:T(8,128)(2,1)S(1)}, u32[]{:S(2)}, u32[]{:S(2)}) collective-permute-start(bf16[16,4096]{1,0:T(8,128)(2,1)S(1)} %get-tuple-element.20), channel_id=1, source_target_pairs={{2,3},{6,7},{10,11},{14,15},{18,19},{22,23},{26,27},{30,31}} | collective-permute-start | bytes 393224 | tf_op jit(solution)/shard_map/ppermute | solution.py:201
  35.6 13.4 %collective-permute-start.7 = (bf16[16,4096]{1,0:T(8,128)(2,1)S(1)}, bf16[16,4096]{1,0:T(8,128)(2,1)S(1)}, u32[]{:S(2)}, u32[]{:S(2)}) collective-permute-start(bf16[16,4096]{1,0:T(8,128)(2,1)S(1)} %fusion.6), channel_id=1, source_target_pairs={{1,0},{5,4},{9,8},{13,12},{17,16},{21,20},{25,24},{29,28}} | collective-permute-start | bytes 393224 | tf_op jit(solution)/shard_map/ppermute | solution.py:203
  38.2 54.6 %collective-permute-start.1 = (bf16[128,4096]{1,0:T(8,128)(2,1)S(1)}, bf16[128,4096]{1,0:T(8,128)(2,1)}, u32[]{:S(2)}, u32[]{:S(2)}) collective-permute-start(bf16[128,4096]{1,0:T(8,128)(2,1)S(1)} %copy-done.2), channel_id=1, source_target_pairs={{0,1},{1,2},{2,3},{3,4},{4,5},{5,6},{6,7},{7,8},{8,9},{9,10},{10,1... | collective-permute-start | bytes 3145736 | tf_op jit(solution)/shard_map/ppermute | solution.py:181
  49.2 42.7 %collective-permute-start.8 = (bf16[16,4096]{1,0:T(8,128)(2,1)S(1)}, bf16[16,4096]{1,0:T(8,128)(2,1)S(1)}, u32[]{:S(2)}, u32[]{:S(2)}) collective-permute-start(bf16[16,4096]{1,0:T(8,128)(2,1)S(1)} %add_convert_fusion), channel_id=1, source_target_pairs={{0,4},{4,8},{8,12},{12,16},{16,20},{20,24},{24,28},{1,5},{5,9},{9,... | collective-permute-start | bytes 393224 | tf_op jit(solution)/shard_map/ppermute | solution.py:213
  76.9 14.9 %collective-permute-start.9 = (bf16[16,4096]{1,0:T(8,128)(2,1)S(1)}, bf16[16,4096]{1,0:T(8,128)(2,1)S(1)}, u32[]{:S(2)}, u32[]{:S(2)}) collective-permute-start(bf16[16,4096]{1,0:T(8,128)(2,1)S(1)} %add_convert_fusion), channel_id=1, source_target_pairs={{0,8},{4,12},{8,16},{12,20},{16,24},{20,28},{1,9},{5,13},{9,17},{1... | collective-permute-start | bytes 393224 | tf_op jit(solution)/shard_map/ppermute | solution.py:213

commit v6 on v5

--- a/solution.py
+++ b/solution.py
@@ -158,7 +158,7 @@
         jnp.bfloat16
     )
     taps = jnp.repeat(short_taps, GROUP, axis=2)
-    rates_wide = lax.optimization_barrier(jnp.repeat(decay_rates, GROUP, axis=1))
+    rates_wide = jnp.repeat(decay_rates, GROUP, axis=1)
 
     smem = pl.BlockSpec(memory_space=pltpu.SMEM)
     tile = lambda part=0: block((rows, TILE), lambda i: (0, i + part * tiles))

time: 103 us -> 115 us (1.12)
  local copies, waits for them, and re-layouts: 8.72 us -> 19.5 us
  other arithmetic: 8.95 us -> 12 us
    select_n x0 -> x5, local copies, waits for them, and re-layouts: none -> 7.79 us  [faded(): jnp.where(alive, jnp.exp(-rates_wide * (distance * jnp.float32(rows))), 0.0)]
    broadcast_in_dim x1 -> x5, local copies, waits for them, and re-layouts: 0.6 us -> 3.74 us  [per_device(): rates_wide = jnp.repeat(decay_rates, GROUP, axis=1)]
    ppermute x1, starting transfers between devices: 10.8 us -> 7.71 us  [per_device(): before = lax.ppermute(product, everyone, pairs)]
    ppermute x2, starting transfers between devices: 30.9 us -> 32.7 us  [per_device(): lax.ppermute(whole, 'ctx', [(i, i + hop) for i in range(ctx_count - hop)])]
    reshape x1 -> x0, local copies, waits for them, and re-layouts: 1.56 us -> none  [per_device(): jnp.repeat(decay_rates, GROUP, axis=1)]
    select_n x0 -> x1, other arithmetic: none -> 1.38 us  [faded(): jnp.where(alive, jnp.exp(-rates_wide * (distance * jnp.float32(rows))), 0.0)]
    convert_element_type x3, other arithmetic: 0.23 us -> 1.47 us  [per_device(): rest.astype(jnp.bfloat16)]
  transfers between devices with their start and end apart: 10 -> 10, of which waited for: 1 -> 0; matrix products, arithmetic and copies ran while one was open for 15% -> 24% of each run, Pallas kernels for 9% -> 8%
where the time goes in v6:
time: 115 us; the launch traced here: 114 us
  starting transfers between devices  51.6 us (45%)
  Pallas kernels  27.5 us (24%)
  local copies, waits for them, and re-layouts  19.5 us (17%)
  other arithmetic  12 us (10%)
  between operations  3.48 us (3%)
    ppermute x2, starting transfers between devices, per_device(): lax.ppermute(whole, 'ctx', [(i, i + hop) for i in range(ctx_count - hop)])  32.7 us
    pallas_call x1, Pallas kernels, per_device(): pl.pallas_call(local_kernel, grid=(tiles,), in_specs=[smem, smem, tile(),...  9.59 us
    pallas_call x1, Pallas kernels, per_device(): pl.pallas_call(final_kernel, grid=(tiles,), in_specs=[smem, smem, tile(),...  9.08 us
    pallas_call x1, Pallas kernels, per_device(): pl.pallas_call(product_kernel, grid=(tiles,), in_specs=[smem, smem, tile(...  8.8 us
    select_n x5, local copies, waits for them, and re-layouts, faded(): jnp.where(alive, jnp.exp(-rates_wide * (distance * jnp.float32(rows))), 0.0)  7.79 us
    ppermute x1, starting transfers between devices, per_device(): before = lax.ppermute(product, everyone, pairs)  7.71 us
    ppermute x3, starting transfers between devices, per_device(): got = lax.ppermute(running.astype(jnp.bfloat16), 'ts', [(hop, hop + 1)])  4.55 us
    ppermute x1, starting transfers between devices, per_device(): edges = lax.ppermute(projected[rows - EDGE:], everyone, pairs)  4.03 us
  transfers between devices with their start and end apart: 10, of which 0 were waited for; matrix products, arithmetic and copies ran while one was open for 24% of the time, Pallas kernels for 8%

profile of v6, /device:TPU:1, one launch (start us, length us, event | category | flops | bytes accessed | tf_op | source)
XLA Modules:
  0.0 114.0 jit_solution(15426249646615224695)
XLA Ops:
  0.0 0.9 slice.9
  0.9 4.0 %collective-permute-start = (bf16[8,12288]{1,0:T(8,128)(2,1)S(1)}, bf16[8,12288]{1,0:T(8,128)(2,1)S(1)}, u32[]{:S(2)}, u32[]{:S(2)}) collective-permute-start(bf16[8,12288]{1,0:T(8,128)(2,1)S(1)} %slice.9), channel_id=1, source_target_pairs={{0,1},{1,2},{2,3},{3,4},{4,5},{5,6},{6,7},{7,8},{8,9},{9,10},{10,1... | collective-permute-start | bytes 589832 | tf_op jit(solution)/shard_map/ppermute | solution.py:141
  5.0 0.7 copy.20
  5.8 0.1 reduce
  5.9 1.4 %fusion.9 = (s32[]{:T(128)}, s32[]{:T(128)}, s32[]{:T(128)}) fusion(s32[]{:T(128)S(6)} %sub.46, s32[16]{0:T(128)S(1)} %reduce, s32[16]{0:T(128)} %lengths.5, s32[]{:T(128)S(6)} %sub.49, s32[]{:T(128)S(6)} %max.3), kind=kLoop, calls=%fused_computation.32 | loop fusion | flops 157 | bytes 152 | tf_op jit(solution)/shard_map/reduce_max | solution.py:187
  10.4 1.4 %exponential_select_fusion.3 = (f32[16,256]{1,0:T(8,128)}, f32[256,16]{0,1:T(8,128)S(1)}, f32[16,256]{1,0:T(8,128)S(1)}, f32[16,256]{1,0:T(8,128)S(1)}, f32[16,2...) fusion(f32[]{:T(128)S(6)} %mul.164, pred[]{:T(512)S(6)} %le.31, f32[16,256]{1,0:T(8,128)} %param.11, ...), kind=kLoop, calls=%fused_computation.21 | loop fusion | flops 57344 | bytes 163861 | tf_op jit(solution)/shard_map/jit(_where)/select_n | solution.py:190
  11.8 0.1 copy.16
  11.9 0.1 neg.34
  12.0 1.5 %exponential_convert_fusion.tail = bf16[4096,128]{1,0:T(8,128)(2,1)} fusion(f32[128]{0:T(128)S(1)} %iota_subtract_fusion, f32[4096]{0:T(1024)S(1)} %neg.34), kind=kLoop, calls=%fused_computation.2 | loop fusion | flops 1048576 | bytes 1065472 | tf_op jit(solution)/shard_map/convert_element_type | solution.py:156
  13.5 1.5 %broadcast_in_dim.40 = f32[3,7,256,16]{3,2,1,0:T(8,128)S(1)} broadcast(f32[3,7,256]{2,1,0:T(8,128)} %param.9), dimensions={0,1,2} | broadcast | bytes 365568 | tf_op jit(solution)/shard_map/broadcast_in_dim | solution.py:160
  15.1 2.5 %reshape.104.taps = f32[3,7,4096]{2,1,0:T(8,128)} reshape(f32[3,7,256,16]{3,2,1,0:T(8,128)S(1)} %broadcast_in_dim.40) | data formatting | bytes 688128 | tf_op jit(solution)/shard_map/reshape | solution.py:160
  17.6 0.0 collective-permute-done.ke_ref.ve_ref.qe_ref
  17.6 0.7 copy-done.1
  18.2 8.8 %product.1 = (bf16[128,4096]{1,0:T(8,128)(2,1)}, f32[16,4096]{1,0:T(8,128)}) custom-call(s32[16]{0:T(128)} %lengths.5, s32[1]{0:T(128)} %bitcast.begin, bf16[128,12288]{1,0:T(8,128)(2,1)} %q_ref.1, bf16[128,12288]{1,0:T(8,128)(2,1)} %q_ref.1, bf16[8,12288]{1,0:T(8,128)(2,1)} %copy-done.1, bf16[8,12288]{1,0:T(8,128)(2,1)} %copy-done.1, ...), custom_call_target="tpu_custom_call" | custom-call | tf_op jit(solution)/shard_map/product/pallas_call | solution.py:170
  27.1 1.0 convert_element_type.69
  28.0 3.2 %collective-permute-start.2 = (bf16[16,4096]{1,0:T(8,128)(2,1)S(1)}, bf16[16,4096]{1,0:T(8,128)(2,1)S(1)}, u32[]{:S(2)}, u32[]{:S(2)}) collective-permute-start(bf16[16,4096]{1,0:T(8,128)(2,1)S(1)} %convert_element_type.69), channel_id=1, source_target_pairs={{0,1},{4,5},{8,9},{12,13},{16,17},{20,21},{24,25},{28,29}} | collective-permute-start | bytes 393224 | tf_op jit(solution)/shard_map/ppermute | solution.py:201
  31.2 0.0 copy-start
  31.2 0.6 broadcast_in_dim.43
  31.8 1.6 %select_n.76 = f32[16,4096]{1,0:T(8,128)S(1)} reshape(f32[16,256,16]{2,1,0:T(8,128)S(1)} %broadcast_in_dim.43) | data formatting | bytes 524288 | tf_op jit(solution)/shard_map/jit(_where)/select_n | solution.py:190
  33.4 0.0 collective-permute-done.2
  33.4 0.0 copy-done
  33.5 0.7 collective-permute-start.3
  34.1 0.6 broadcast_in_dim.45
  34.7 1.6 %select_n.84 = f32[16,4096]{1,0:T(8,128)S(1)} reshape(f32[16,256,16]{2,1,0:T(8,128)S(1)} %broadcast_in_dim.45) | data formatting | bytes 524288 | tf_op jit(solution)/shard_map/jit(_where)/select_n | solution.py:190
  36.3 0.0 collective-permute-done.3
  36.3 0.7 fusion.13
  37.0 0.7 collective-permute-start.5
  37.7 0.8 copy.19
  38.5 0.1 mul.153
  38.6 0.0 collective-permute-done.5
  38.6 0.7 fusion.4
  39.3 0.7 collective-permute-start.6
  40.0 1.4 %multiply_convert_fusion.decay = bf16[128,4096]{1,0:T(8,128)(2,1)} fusion(f32[128]{0:T(128)S(1)} %iota_add_fusion, f32[4096]{0:T(1024)S(1)} %neg.34, f32[4096]{0:T(1024)S(1)} %mul.153), kind=kLoop, calls=%fused_computation.1 | loop fusion | flops 1572864 | bytes 1081856 | tf_op jit(solution)/shard_map/convert_element_type | solution.py:157
  41.4 0.0 copy-done.2
  41.4 0.0 slice-start
  41.4 0.0 copy-start.3
  41.4 1.3 %broadcast_in_dim.46 = f32[16,256,16]{2,1,0:T(8,128)S(1)} broadcast(f32[16,256]{1,0:T(8,128)} %get-tuple-element.25), dimensions={0,1} | broadcast | bytes 278528 | tf_op jit(solution)/shard_map/broadcast_in_dim | solution.py:161
  42.8 1.6 %select_n.87 = f32[16,4096]{1,0:T(8,128)S(1)} reshape(f32[16,256,16]{2,1,0:T(8,128)S(1)} %broadcast_in_dim.46) | data formatting | bytes 524288 | tf_op jit(solution)/shard_map/jit(_where)/select_n | solution.py:190
  44.3 0.1 copy.21
  44.4 0.0 copy-start.5
  44.4 0.2 rev.3
  44.6 0.0 slice-done
  44.6 0.1 copy.18
  44.8 0.7 collective-permute-start.4
  45.5 0.0 collective-permute-done.6
  45.6 1.3 %collective-permute-start.7 = (bf16[16,4096]{1,0:T(8,128)(2,1)S(1)}, bf16[16,4096]{1,0:T(8,128)(2,1)S(1)}, u32[]{:S(2)}, u32[]{:S(2)}) collective-permute-start(bf16[16,4096]{1,0:T(8,128)(2,1)S(1)} %fusion.5), channel_id=1, source_target_pairs={{1,0},{5,4},{9,8},{13,12},{17,16},{21,20},{25,24},{29,28}} | collective-permute-start | bytes 393224 | tf_op jit(solution)/shard_map/ppermute | solution.py:203
  46.9 2.0 %multiply_reduce_fusion = f32[256,128]{1,0:T(8,128)S(1)} fusion(f32[128]{0:T(128)S(1)} %fusion.7, f32[16,256]{1,0:T(8,128)} %get-tuple-element.28, f32[16,256]{1,0:T(8,128)} %get-tuple-element.27), kind=kLoop, calls=%fused_computation | loop fusion | flops 1540096 | bytes 164352 | tf_op jit(solution)/shard_map/reduce_sum | solution.py:150
  48.8 7.7 %collective-permute-start.1 = (bf16[128,4096]{1,0:T(8,128)(2,1)}, bf16[128,4096]{1,0:T(8,128)(2,1)}, u32[]{:S(2)}, u32[]{:S(2)}) collective-permute-start(bf16[128,4096]{1,0:T(8,128)(2,1)} %get-tuple-element.9.x_ref), channel_id=1, source_target_pairs={{0,1},{1,2},{2,3},{3,4},{4,5},{5,6},{6,7},{7,8},{8,9},{9,10},{10,1... | collective-permute-start | bytes 3145736 | tf_op jit(solution)/shard_map/ppermute | solution.py:181
  56.5 0.0 collective-permute-done.4
  56.6 0.0 collective-permute-done.7
  56.6 0.1 add_convert_fusion
  56.7 29.6 %collective-permute-start.8 = (bf16[16,4096]{1,0:T(8,128)(2,1)S(1)}, bf16[16,4096]{1,0:T(8,128)(2,1)S(1)}, u32[]{:S(2)}, u32[]{:S(2)}) collective-permute-start(bf16[16,4096]{1,0:T(8,128)(2,1)S(1)} %add_convert_fusion), channel_id=1, source_target_pairs={{0,4},{4,8},{8,12},{12,16},{16,20},{20,24},{24,28},{1,5},{5,9},{9,... | collective-permute-start | bytes 393224 | tf_op jit(solution)/shard_map/ppermute | solution.py:213
  86.3 3.1 %collective-permute-start.9 = (bf16[16,4096]{1,0:T(8,128)(2,1)S(1)}, bf16[16,4096]{1,0:T(8,128)(2,1)S(1)}, u32[]{:S(2)}, u32[]{:S(2)}) collective-permute-start(bf16[16,4096]{1,0:T(8,128)(2,1)S(1)} %add_convert_fusion), channel_id=1, source_target_pairs={{0,8},{4,12},{8,16},{12,20},{16,24},{20,28},{1,9},{5,13},{9,17},{1... | collective-permute-start | bytes 393224 | tf_op jit(solution)/shard_map/ppermute | solution.py:213
  89.4 0.8 fusion.12
  90.2 0.6 broadcast_in_dim.44
  90.8 1.6 %select_n.80 = f32[16,4096]{1,0:T(8,128)S(1)} reshape(f32[16,256,16]{2,1,0:T(8,128)S(1)} %broadcast_in_dim.44) | data formatting | bytes 524288 | tf_op jit(solution)/shard_map/jit(_where)/select_n | solution.py:190
  92.4 0.6 broadcast_in_dim.47
  93.0 1.6 %select_n.90 = f32[16,4096]{1,0:T(8,128)S(1)} reshape(f32[16,256,16]{2,1,0:T(8,128)S(1)} %broadcast_in_dim.47) | data formatting | bytes 524288 | tf_op jit(solution)/shard_map/jit(_where)/select_n | solution.py:190
  94.5 9.6 %local.1 = (f32[128,4096]{1,0:T(8,128)}, f32[128,4096]{1,0:T(8,128)}) custom-call(s32[16]{0:T(128)} %lengths.5, s32[1]{0:T(128)} %bitcast.begin, bf16[128,4096]{1,0:T(8,128)(2,1)} %get-tuple-element.9.x_ref, bf16[128,12288]{1,0:T(8,128)(2,1)} %q_ref.1, bf16[8,12288]{1,0:T(8,128)(2,1)} %copy-done.1, f32[3,7,4096]{2,1,0:T(8,128)} %reshape.104.taps, ...), custom_call_target="tpu_custom_call" | custom-call | flops 1073741824 | bytes 6291456 | tf_op jit(solution)/shard_map/local/pallas_call | solution.py:218
  104.1 0.0 collective-permute-done.8
  104.1 0.0 collective-permute-done.9
  104.1 0.8 multiply_add_fusion.state
  104.9 0.0 collective-permute-done.1.x_ref
  104.9 9.1 %final.1 = bf16[128,4096]{1,0:T(8,128)(2,1)} custom-call(s32[16]{0:T(128)} %lengths.5, s32[1]{0:T(128)} %bitcast.begin, bf16[128,4096]{1,0:T(8,128)(2,1)} %collective-permute-done.1.x_ref, f32[256,128]{1,0:T(8,128)} %get-tuple-element.17.wheel, bf16[128,4096]{1,0:T(8,128)(2,1)} %multiply_convert_fusion.decay, f32[16,4096]{1,0:T(8,128)} %multiply_add_fusion.state, ...), custom_call_target="tpu_custom_call" | custom-call | tf_op jit(solution)/shard_map/final/pallas_call | solution.py:235
  (13 shorter events, 0.2 us)
Async XLA Ops:
  0.9 16.6 %collective-permute-start = (bf16[8,12288]{1,0:T(8,128)(2,1)S(1)}, bf16[8,12288]{1,0:T(8,128)(2,1)S(1)}, u32[]{:S(2)}, u32[]{:S(2)}) collective-permute-start(bf16[8,12288]{1,0:T(8,128)(2,1)S(1)} %slice.9), channel_id=1, source_target_pairs={{0,1},{1,2},{2,3},{3,4},{4,5},{5,6},{6,7},{7,8},{8,9},{9,10},{10,1... | collective-permute-start | bytes 589832 | tf_op jit(solution)/shard_map/ppermute | solution.py:141
  17.6 0.7 copy-start.1
  28.0 5.4 %collective-permute-start.2 = (bf16[16,4096]{1,0:T(8,128)(2,1)S(1)}, bf16[16,4096]{1,0:T(8,128)(2,1)S(1)}, u32[]{:S(2)}, u32[]{:S(2)}) collective-permute-start(bf16[16,4096]{1,0:T(8,128)(2,1)S(1)} %convert_element_type.69), channel_id=1, source_target_pairs={{0,1},{4,5},{8,9},{12,13},{16,17},{20,21},{24,25},{28,29}} | collective-permute-start | bytes 393224 | tf_op jit(solution)/shard_map/ppermute | solution.py:201
  31.2 2.2 %copy-start = (f32[16,4096]{1,0:T(8,128)S(1)}, f32[16,4096]{1,0:T(8,128)}, u32[]{:S(2)}) copy-start(f32[16,4096]{1,0:T(8,128)} %get-tuple-element.10) | copy-start | bytes 786436
  33.5 2.8 %collective-permute-start.3 = (bf16[16,4096]{1,0:T(8,128)(2,1)S(1)}, bf16[16,4096]{1,0:T(8,128)(2,1)S(1)}, u32[]{:S(2)}, u32[]{:S(2)}) collective-permute-start(bf16[16,4096]{1,0:T(8,128)(2,1)S(1)} %fusion.6), channel_id=1, source_target_pairs={{1,2},{5,6},{9,10},{13,14},{17,18},{21,22},{25,26},{29,30}} | collective-permute-start | bytes 393224 | tf_op jit(solution)/shard_map/ppermute | solution.py:201
  36.3 5.1 %copy-start.2 = (f32[128,256]{1,0:T(8,128)S(1)}, f32[128,256]{1,0:T(8,128)}, u32[]{:S(2)}) copy-start(f32[128,256]{1,0:T(8,128)} %param.10) | copy-start | bytes 393220
  37.0 1.6 %collective-permute-start.5 = (bf16[16,4096]{1,0:T(8,128)(2,1)S(1)}, bf16[16,4096]{1,0:T(8,128)(2,1)S(1)}, u32[]{:S(2)}, u32[]{:S(2)}) collective-permute-start(bf16[16,4096]{1,0:T(8,128)(2,1)S(1)} %get-tuple-element.18), channel_id=1, source_target_pairs={{3,2},{7,6},{11,10},{15,14},{19,18},{23,22},{27,26},{31,30}} | collective-permute-start | bytes 393224 | tf_op jit(solution)/shard_map/ppermute | solution.py:203
  39.3 6.2 %collective-permute-start.6 = (bf16[16,4096]{1,0:T(8,128)(2,1)}, bf16[16,4096]{1,0:T(8,128)(2,1)S(1)}, u32[]{:S(2)}, u32[]{:S(2)}) collective-permute-start(bf16[16,4096]{1,0:T(8,128)(2,1)} %fusion.4), channel_id=1, source_target_pairs={{2,1},{6,5},{10,9},{14,13},{18,17},{22,21},{26,25},{30,29}} | collective-permute-start | bytes 393224 | tf_op jit(solution)/shard_map/ppermute | solution.py:203
  41.4 3.2 %slice-start = ((f32[128,256]{1,0:T(8,128)}), f32[1,256]{1,0:T(1,128)S(1)}, s32[]{:S(2)}) async-start(f32[128,256]{1,0:T(8,128)} %param.10), calls=%async_computation | async-start | bytes 2048 | tf_op jit(solution)/shard_map/slice | solution.py:149
  41.4 3.4 %copy-start.3 = (bf16[16,4096]{1,0:T(8,128)(2,1)S(1)}, bf16[16,4096]{1,0:T(8,128)(2,1)}, u32[]{:S(2)}) copy-start(bf16[16,4096]{1,0:T(8,128)(2,1)} %get-tuple-element.20) | copy-start | bytes 393220
  44.4 45.8 %copy-start.5 = (f32[16,256]{1,0:T(8,128)S(1)}, f32[16,256]{1,0:T(8,128)}, u32[]{:S(2)}) copy-start(f32[16,256]{1,0:T(8,128)} %get-tuple-element.21) | copy-start | bytes 49156
  44.8 11.7 %collective-permute-start.4 = (bf16[16,4096]{1,0:T(8,128)(2,1)S(1)}, bf16[16,4096]{1,0:T(8,128)(2,1)S(1)}, u32[]{:S(2)}, u32[]{:S(2)}) collective-permute-start(bf16[16,4096]{1,0:T(8,128)(2,1)S(1)} %copy-done.3), channel_id=1, source_target_pairs={{2,3},{6,7},{10,11},{14,15},{18,19},{22,23},{26,27},{30,31}} | collective-permute-start | bytes 393224 | tf_op jit(solution)/shard_map/ppermute | solution.py:201
  45.6 11.0 %collective-permute-start.7 = (bf16[16,4096]{1,0:T(8,128)(2,1)S(1)}, bf16[16,4096]{1,0:T(8,128)(2,1)S(1)}, u32[]{:S(2)}, u32[]{:S(2)}) collective-permute-start(bf16[16,4096]{1,0:T(8,128)(2,1)S(1)} %fusion.5), channel_id=1, source_target_pairs={{1,0},{5,4},{9,8},{13,12},{17,16},{21,20},{25,24},{29,28}} | collective-permute-start | bytes 393224 | tf_op jit(solution)/shard_map/ppermute | solution.py:203
  48.8 56.1 %collective-permute-start.1 = (bf16[128,4096]{1,0:T(8,128)(2,1)}, bf16[128,4096]{1,0:T(8,128)(2,1)}, u32[]{:S(2)}, u32[]{:S(2)}) collective-permute-start(bf16[128,4096]{1,0:T(8,128)(2,1)} %get-tuple-element.9.x_ref), channel_id=1, source_target_pairs={{0,1},{1,2},{2,3},{3,4},{4,5},{5,6},{6,7},{7,8},{8,9},{9,10},{10,1... | collective-permute-start | bytes 3145736 | tf_op jit(solution)/shard_map/ppermute | solution.py:181
  56.7 47.4 %collective-permute-start.8 = (bf16[16,4096]{1,0:T(8,128)(2,1)S(1)}, bf16[16,4096]{1,0:T(8,128)(2,1)S(1)}, u32[]{:S(2)}, u32[]{:S(2)}) collective-permute-start(bf16[16,4096]{1,0:T(8,128)(2,1)S(1)} %add_convert_fusion), channel_id=1, source_target_pairs={{0,4},{4,8},{8,12},{12,16},{16,20},{20,24},{24,28},{1,5},{5,9},{9,... | collective-permute-start | bytes 393224 | tf_op jit(solution)/shard_map/ppermute | solution.py:213
  86.3 17.9 %collective-permute-start.9 = (bf16[16,4096]{1,0:T(8,128)(2,1)S(1)}, bf16[16,4096]{1,0:T(8,128)(2,1)S(1)}, u32[]{:S(2)}, u32[]{:S(2)}) collective-permute-start(bf16[16,4096]{1,0:T(8,128)(2,1)S(1)} %add_convert_fusion), channel_id=1, source_target_pairs={{0,8},{4,12},{8,16},{12,20},{16,24},{20,28},{1,9},{5,13},{9,17},{1... | collective-permute-start | bytes 393224 | tf_op jit(solution)/shard_map/ppermute | solution.py:213
  90.2 2.2 %copy-start.4 = (f32[16,256]{1,0:T(8,128)S(1)}, f32[16,256]{1,0:T(8,128)}, u32[]{:S(2)}) copy-start(f32[16,256]{1,0:T(8,128)} %get-tuple-element.26) | copy-start | bytes 49156
